TPU v7x, 256 devices: a whole 4x4x8 slice. The times are simulated.
256 devices in a mesh: gx: 8 (over z), gy: 8 (over x, core), gz: 4 (over y).
Axes of the slice: x: 4, y: 4, z: 8, core: 2. Of those that a mesh axis runs over, the one named last changes fastest.
Arguments:
- velocity: float32 [2, 32, 512, 1024], P(None, 'gz', 'gx', 'gy'), may hold values from -6 to 6
- viscosity: float32 [32, 512, 1024], P('gz', 'gx', 'gy'), may hold values from 0.3 to 3
- block_inverse: float32 [3, 32, 512, 1024], P(None, 'gz', 'gx', 'gy'), may hold values from -0.05 to 1, as said below
- coupling: float32 [32, 512, 1024], P('gz', 'gx', 'gy'), may hold values from 0.85 to 1
- friction: float32 [512, 1024], P('gx', 'gy'), may hold values from 0.5 to 5
- friction_step: float32 [512, 1024], P('gx', 'gy'), may hold values from -6 to 6
- misfit_weight: float32 [512, 1024], P('gx', 'gy'), may hold values from 0.5 to 2
- ice_tiles: int32 [32, 64], P('gx', 'gy'), may hold values 0 or 1
- bed_layer: int32 [512, 1024], P('gx', 'gy'), may hold values from 0 to 30
Outputs:
- increment: float32 [2, 32, 512, 1024], P(None, 'gz', 'gx', 'gy')
- adjoint: float32 [2, 32, 512, 1024], P(None, 'gz', 'gx', 'gy')
- hessian_action: float32 [512, 1024], P('gx', 'gy')
Inputs may be any that keep to these rules, and one draw needn't show every extreme that they name: For every cell the block [[block_inverse[0], block_inverse[1]], [block_inverse[1], block_inverse[2]]] is symmetric positive definite, its diagonal entries at least 0.85 and its off-diagonal entry at most 0.05 in magnitude.
All inputs are finite; a program needn't handle non-finite values. No bound on the sum of `ice_tiles` on one device may be relied on, other than what follows from the above.
Results may differ from a plain program's by a relative error of at most 0.0001.
Values sent between devices are 32-bit elements; how exact they have to be, the bound alone decides.
A program may use at most 64 MiB of HBM per device.

v0:
```python
import jax
import jax.numpy as jnp
from jax import lax
from jax.sharding import PartitionSpec as P

TILE = 16
ITERS = 2


VERTICAL = 8.0
STRETCH = 4.0


def with_halo(block, sides, width):
    for axis, dim in sides:
        count = lax.axis_size(axis)
        forward = [(i, i + 1) for i in range(count - 1)]
        backward = [(target, source) for source, target in forward]
        low = lax.ppermute(
            lax.slice_in_dim(block, block.shape[dim] - width, None, axis=dim), axis, forward
        )
        high = lax.ppermute(lax.slice_in_dim(block, 0, width, axis=dim), axis, backward)
        block = jnp.concatenate([low, block, high], axis=dim)
    return block


def from_behind(array, axis, by):
    count = lax.axis_size(axis)
    pairs = [(i, i + by) for i in range(count) if 0 <= i + by < count]
    return lax.ppermute(array, axis, pairs)


def neighbor_slices():
    inner = slice(1, -1)
    return [
        (slice(2, None), inner, inner),
        (slice(None, -2), inner, inner),
        (inner, slice(2, None), inner),
        (inner, slice(None, -2), inner),
        (inner, inner, slice(2, None)),
        (inner, inner, slice(None, -2)),
    ]


def face_weights(padded_eta, padded_act):
    centre = (slice(1, -1), slice(1, -1), slice(1, -1))
    centre_eta = padded_eta[centre]
    centre_act = padded_act[centre]
    result = []
    for position, slices in enumerate(neighbor_slices()):
        factor = VERTICAL if position < 2 else 1.0
        result.append(
            factor * 0.5 * (centre_eta + padded_eta[slices]) * centre_act * padded_act[slices]
        )
    return result


def apply_operator(field, weights, diagonal):
    padded = with_halo(field, (("gx", 2), ("gy", 3), ("gz", 1)), 1)
    stretch_x = jnp.array([STRETCH, 1.0], jnp.float32).reshape(2, 1, 1, 1)
    stretch_y = jnp.array([1.0, STRETCH], jnp.float32).reshape(2, 1, 1, 1)
    nbrs = [padded[(slice(None),) + slices] for slices in neighbor_slices()]
    vertical = weights[0] * nbrs[0] + weights[1] * nbrs[1]
    east_west = weights[2] * nbrs[2] + weights[3] * nbrs[3]
    north_south = weights[4] * nbrs[4] + weights[5] * nbrs[5]
    return diagonal * field - vertical - stretch_x * east_west - stretch_y * north_south


def sym_apply(block, vector):
    return jnp.stack(
        [block[0] * vector[0] + block[1] * vector[1], block[1] * vector[0] + block[2] * vector[1]]
    )


def full_apply(matrix, vector):
    return jnp.stack(
        [
            matrix[0] * vector[0] + matrix[1] * vector[1],
            matrix[2] * vector[0] + matrix[3] * vector[1],
        ]
    )


def full_compose(latter, earlier):
    return jnp.stack(
        [
            latter[0] * earlier[0] + latter[1] * earlier[2],
            latter[0] * earlier[1] + latter[1] * earlier[3],
            latter[2] * earlier[0] + latter[3] * earlier[2],
            latter[2] * earlier[1] + latter[3] * earlier[3],
        ]
    )


def sym_to_full(block):
    return jnp.stack([block[0], block[1], block[1], block[2]])


def chain_carry(mapping, offset, upward):
    blank = jnp.zeros_like(offset)
    incoming = blank
    for turn_index in range(lax.axis_size("gz") - 1):
        outgoing = full_apply(mapping, incoming) + offset
        if upward:
            incoming = from_behind(outgoing, "gz", 1)
        else:
            incoming = from_behind(outgoing, "gz", -1)
    return incoming


def precondition(residual, inverse, coupled, unit_map):
    depth = coupled.shape[0]
    scaled = coupled[None] * inverse
    sources = sym_apply(inverse, residual)
    mapping = unit_map
    offset = jnp.zeros_like(sources[:, 0])
    for index in range(depth):
        layer_map = sym_to_full(scaled[:, index])
        mapping = full_compose(layer_map, mapping)
        offset = full_apply(layer_map, offset) + sources[:, index]
    incoming = chain_carry(mapping, offset, True)
    upward = []
    for index in range(depth):
        incoming = sym_apply(scaled[:, index], incoming) + sources[:, index]
        upward.append(incoming)
    mapping = unit_map
    offset = jnp.zeros_like(sources[:, 0])
    for index in reversed(range(depth)):
        layer_map = sym_to_full(scaled[:, index])
        mapping = full_compose(layer_map, mapping)
        offset = full_apply(layer_map, offset) + coupled[index] * upward[index]
    incoming = chain_carry(mapping, offset, False)
    settled = [None] * depth
    for index in reversed(range(depth)):
        value = upward[index] + sym_apply(inverse[:, index], incoming)
        settled[index] = value
        incoming = coupled[index] * value
    return jnp.stack(settled, axis=1)


def norm_total(residual, precond):
    return lax.psum(jnp.sum(residual * precond), ("gx", "gy", "gz"))


def curvature_total(direction, image):
    return lax.psum(jnp.sum(direction * image), ("gx", "gy", "gz"))


def solve(rhs, operator, precond_fn):
    solution = jnp.zeros_like(rhs)
    residual = rhs
    precond = precond_fn(residual)
    direction = precond
    energy = norm_total(residual, precond)
    for iteration in range(ITERS):
        image = operator(direction)
        step_length = energy / curvature_total(direction, image)
        solution = solution + step_length * direction
        residual = residual - step_length * image
        if iteration + 1 < ITERS:
            precond = precond_fn(residual)
            renewed = norm_total(residual, precond)
            direction = precond + renewed / energy * direction
            energy = renewed
    return solution


def local(
    velocity,
    viscosity,
    block_inverse,
    coupling,
    friction,
    friction_step,
    misfit_weight,
    ice_tiles,
    bed_layer,
):
    depth = viscosity.shape[0]
    column = jnp.repeat(jnp.repeat(ice_tiles, TILE, axis=0), TILE, axis=1).astype(jnp.float32)
    levels = (lax.axis_index("gz") * depth + jnp.arange(depth, dtype=jnp.int32)).reshape(
        depth, 1, 1
    )
    top_level = lax.axis_size("gz") * depth - 1
    active = column[None] * (levels >= bed_layer[None]).astype(jnp.float32)
    beneath = column[None] * (levels - 1 >= bed_layer[None]).astype(jnp.float32)
    bedflag = column[None] * (levels == bed_layer[None]).astype(jnp.float32)
    surface = column[None] * (levels == top_level).astype(jnp.float32)
    padded = with_halo(jnp.stack([viscosity, active]), (("gx", 2), ("gy", 3), ("gz", 1)), 1)
    weights = face_weights(padded[0], padded[1])
    stretch_x = jnp.array([STRETCH, 1.0], jnp.float32).reshape(2, 1, 1, 1)
    stretch_y = jnp.array([1.0, STRETCH], jnp.float32).reshape(2, 1, 1, 1)
    diagonal = (
        weights[0]
        + weights[1]
        + stretch_x * (weights[2] + weights[3])
        + stretch_y * (weights[4] + weights[5])
        + friction * bedflag
        + (1.0 - active)
    )
    inverse = jnp.stack(
        [
            active * block_inverse[0] + (1.0 - active),
            active * block_inverse[1],
            active * block_inverse[2] + (1.0 - active),
        ]
    )
    coupled = coupling * active * beneath
    ones_map = jnp.ones_like(friction)
    zeros_map = jnp.zeros_like(friction)
    unit_map = jnp.stack([ones_map, zeros_map, zeros_map, ones_map])

    def operator(field):
        return apply_operator(field, weights, diagonal)

    def precond_fn(field):
        return precondition(field, inverse, coupled, unit_map)

    increment = solve(bedflag * friction * friction_step * velocity, operator, precond_fn)
    adjoint = solve(surface * misfit_weight * increment, operator, precond_fn)
    local_terms = friction * jnp.sum(bedflag * velocity * adjoint, axis=(0, 1))
    hessian_action = lax.psum(local_terms, "gz")
    return (increment, adjoint, hessian_action)


def solution(mesh):
    in_specs = (
        P(None, "gz", "gx", "gy"),
        P("gz", "gx", "gy"),
        P(None, "gz", "gx", "gy"),
        P("gz", "gx", "gy"),
        P("gx", "gy"),
        P("gx", "gy"),
        P("gx", "gy"),
        P("gx", "gy"),
        P("gx", "gy"),
    )
    out_specs = (P(None, "gz", "gx", "gy"), P(None, "gz", "gx", "gy"), P("gx", "gy"))
    return jax.shard_map(local, mesh=mesh, in_specs=in_specs, out_specs=out_specs, check_vma=False)
```

profile of v0, /device:TPU:2, one launch (start us, length us, event | category | flops | bytes accessed | tf_op | source)
XLA Modules:
  0.0 811.7 jit_solution(4926578920875180842)
XLA Ops:
  6.0 3.5 collective-permute-start
  11.4 4.3 collective-permute-start.1
  17.0 4.5 collective-permute-start.6
  21.7 3.5 collective-permute-start.2
  31.6 5.1 collective-permute-done.3
  57.2 5.8 collective-permute-start.10
  66.2 4.5 collective-permute-start.12
  77.2 3.6 collective-permute-start.15
  86.7 3.9 collective-permute-start.17
  93.8 4.4 collective-permute-done.16
  100.0 77.8 %all-reduce.1 = (f32[]{:T(128)}, f32[]{:T(128)}) all-reduce(f32[]{:T(128)} %get-tuple-element.15, f32[]{:T(128)} %get-tuple-element.14), channel_id=1, replica_groups=mesh['gx'=8,'gy'=8,'gz'=4] {'gx','gy','gz'}, use_global_device_ids=true, to_apply=%region_1.0 | all-reduce | flops 2 | bytes 16 | tf_op jit(solution)/shard_map/psum | solution.py:142
  184.0 4.3 collective-permute-start.19
  190.2 4.3 collective-permute-start.20
  199.5 5.2 collective-permute-done.21
  206.1 5.7 collective-permute-done.22
  213.3 4.8 collective-permute-done.23
  219.3 74.1 %psum.65 = f32[]{:T(128)} all-reduce(f32[]{:T(128)} %multiply_reduce_fusion.4), channel_id=1, replica_groups=mesh['gx'=8,'gy'=8,'gz'=4] {'gx','gy','gz'}, use_global_device_ids=true, to_apply=%region_5.0 | all-reduce | flops 1 | bytes 8 | tf_op jit(solution)/shard_map/psum | solution.py:142
  296.1 4.5 collective-permute-start.24
  307.8 3.8 collective-permute-start.27
  320.6 2.8 collective-permute-done.29
  323.4 4.1 collective-permute-done.28
  327.6 3.2 fusion.35
  330.8 73.5 %psum.66 = f32[]{:T(128)} all-reduce(f32[]{:T(128)} %fusion.35), channel_id=1, replica_groups=mesh['gx'=8,'gy'=8,'gz'=4] {'gx','gy','gz'}, use_global_device_ids=true, to_apply=%region_7.0 | all-reduce | flops 1 | bytes 8 | tf_op jit(solution)/shard_map/psum | solution.py:146
  413.5 4.3 collective-permute-start.31
  419.7 4.3 collective-permute-start.32
  429.0 5.4 collective-permute-done.33
  435.7 5.2 collective-permute-done.34
  442.3 4.9 collective-permute-done.35
  448.9 4.5 collective-permute-start.36
  461.8 3.8 collective-permute-start.39
  470.6 3.8 collective-permute-start.41
  475.7 2.8 collective-permute-done.41
  478.5 4.4 collective-permute-done.40
  483.0 4.1 multiply_reduce_fusion.2
  487.1 75.2 %all-reduce = (f32[]{:T(128)}, f32[]{:T(128)}) all-reduce(f32[]{:T(128)} %get-tuple-element.13, f32[]{:T(128)} %get-tuple-element.12), channel_id=1, replica_groups=mesh['gx'=8,'gy'=8,'gz'=4] {'gx','gy','gz'}, use_global_device_ids=true, to_apply=%region_9.0 | all-reduce | flops 2 | bytes 16 | tf_op jit(solution)/shard_map/psum | solution.py:142
  565.9 2.9 collective-permute-start.42
  570.7 4.3 collective-permute-start.43
  576.9 4.3 collective-permute-start.44
  586.2 5.4 collective-permute-done.45
  592.9 5.2 collective-permute-done.46
  599.7 4.6 collective-permute-done.47
  605.5 75.1 %psum.69 = f32[]{:T(128)} all-reduce(f32[]{:T(128)} %multiply_reduce_fusion.1), channel_id=1, replica_groups=mesh['gx'=8,'gy'=8,'gz'=4] {'gx','gy','gz'}, use_global_device_ids=true, to_apply=%region_13.0 | all-reduce | flops 1 | bytes 8 | tf_op jit(solution)/shard_map/psum | solution.py:142
  683.4 4.5 collective-permute-start.48
  695.1 3.8 collective-permute-start.51
  706.9 5.3 collective-permute-done.52
  712.2 2.8 fusion.5
  715.1 74.4 %psum.70 = f32[]{:T(128)} all-reduce(f32[]{:T(128)} %fusion.5), channel_id=1, replica_groups=mesh['gx'=8,'gy'=8,'gz'=4] {'gx','gy','gz'}, use_global_device_ids=true, to_apply=%region_15.0 | all-reduce | flops 1 | bytes 8 | tf_op jit(solution)/shard_map/psum | solution.py:146
  792.9 18.1 %psum.71 = f32[64,128]{0,1:T(8,128)S(1)} all-reduce(f32[64,128]{0,1:T(8,128)S(1)} %mul.8618), channel_id=1, replica_groups=mesh['gx'=8,'gy'=8,'gz'=4] {'gz'}, use_global_device_ids=true, to_apply=%region_17.0 | all-reduce | flops 8192 | bytes 65536 | tf_op jit(solution)/shard_map/psum | solution.py:222
  (842 shorter events, 153.5 us)
Async XLA Ops:
  6.0 5.4 collective-permute-start
  11.4 10.2 %collective-permute-start.1 = (f32[2,64,128]{2,1,0:T(8,128)S(1)}, f32[2,64,128]{2,1,0:T(8,128)S(1)}, u32[]{:S(2)}, u32[]{:S(2)}) collective-permute-start(f32[2,64,128]{2,1,0:T(8,128)S(1)} %maximum_add_fusion.7), channel_id=1, source_target_pairs={{0,1},{1,2},{2,3},{4,5},{5,6},{6,7},{8,9},{9,10},{10,11},{12,13},{... | collective-permute-start | bytes 196616 | tf_op jit(solution)/shard_map/ppermute | solution.py:30
  15.7 15.8 %collective-permute-start.7 = (f32[2,8,1,128]{3,1,2,0:T(8,128)S(1)}, f32[2,8,1,128]{3,1,2,0:T(8,128)S(1)}, u32[]{:S(2)}, u32[]{:S(2)}) collective-permute-start(f32[2,8,1,128]{3,1,2,0:T(8,128)S(1)} %bitcast.1880), channel_id=1, source_target_pairs={{32,0},{64,32},{96,64},{128,96},{160,128},{192,160},{224,192},{33,... | collective-permute-start | bytes 24584 | tf_op jit(solution)/shard_map/ppermute | solution.py:22
  17.0 14.5 %collective-permute-start.6 = (f32[2,8,1,128]{3,1,2,0:T(8,128)S(1)}, f32[2,8,1,128]{3,1,2,0:T(8,128)S(1)}, u32[]{:S(2)}, u32[]{:S(2)}) collective-permute-start(f32[2,8,1,128]{3,1,2,0:T(8,128)S(1)} %bitcast.1879), channel_id=1, source_target_pairs={{0,32},{32,64},{64,96},{96,128},{128,160},{160,192},{192,224},{1,3... | collective-permute-start | bytes 24584 | tf_op jit(solution)/shard_map/ppermute | solution.py:19
  21.7 5.4 collective-permute-start.2
  30.2 6.5 collective-permute-start.3
  37.3 14.1 %collective-permute-start.4 = (f32[2,64,128]{2,1,0:T(8,128)}, f32[2,64,128]{2,1,0:T(8,128)}, u32[]{:S(2)}, u32[]{:S(2)}) collective-permute-start(f32[2,64,128]{2,1,0:T(8,128)} %maximum_add_fusion.25), channel_id=1, source_target_pairs={{1,0},{2,1},{3,2},{5,4},{6,5},{7,6},{9,8},{10,9},{11,10},{13,12},{... | collective-permute-start | bytes 196616 | tf_op jit(solution)/shard_map/ppermute | solution.py:30
  44.2 5.3 collective-permute-start.8
  53.2 9.8 %collective-permute-start.5 = (f32[2,64,128]{2,1,0:T(8,128)S(1)}, f32[2,64,128]{2,1,0:T(8,128)S(1)}, u32[]{:S(2)}, u32[]{:S(2)}) collective-permute-start(f32[2,64,128]{2,1,0:T(8,128)S(1)} %maximum_add_fusion.26), channel_id=1, source_target_pairs={{1,0},{2,1},{3,2},{5,4},{6,5},{7,6},{9,8},{10,9},{11,10},{13,12},{... | collective-permute-start | bytes 196616 | tf_op jit(solution)/shard_map/ppermute | solution.py:30
  55.7 15.0 %collective-permute-start.11 = (f32[2,1,66,130]{3,2,1,0:T(8,128)S(1)}, f32[2,1,66,130]{3,2,1,0:T(8,128)S(1)}, u32[]{:S(2)}, u32[]{:S(2)}) collective-permute-start(f32[2,1,66,130]{3,2,1,0:T(8,128)S(1)} %get-tuple-element.109), channel_id=1, source_target_pairs={{1,0},{2,1},{3,2},{5,4},{6,5},{7,6},{9,8},{10,9},{11,10},{13,12},{... | collective-permute-start | bytes 205928 | tf_op jit(solution)/shard_map/ppermute | solution.py:22
  57.2 13.6 %collective-permute-start.10 = (f32[2,1,66,130]{3,2,1,0:T(8,128)S(1)}, f32[2,1,66,130]{3,2,1,0:T(8,128)S(1)}, u32[]{:S(2)}, u32[]{:S(2)}) collective-permute-start(f32[2,1,66,130]{3,2,1,0:T(8,128)S(1)} %get-tuple-element.108), channel_id=1, source_target_pairs={{0,1},{1,2},{2,3},{4,5},{5,6},{6,7},{8,9},{9,10},{10,11},{12,13},{... | collective-permute-start | bytes 205928 | tf_op jit(solution)/shard_map/ppermute | solution.py:19
  64.9 7.7 collective-permute-start.13
  66.2 6.4 collective-permute-start.12
  75.0 8.2 %collective-permute-start.14 = (f32[2,8,66,1]{2,1,3,0:T(8,128)S(1)}, f32[2,8,66,1]{2,1,3,0:T(8,128)S(1)}, u32[]{:S(2)}, u32[]{:S(2)}) collective-permute-start(f32[2,8,66,1]{2,1,3,0:T(8,128)S(1)} %copy.327), channel_id=1, source_target_pairs={{0,4},{4,8},{8,12},{12,16},{16,20},{20,24},{24,28},{1,5},{5,9},{9,... | collective-permute-start | bytes 12680 | tf_op jit(solution)/shard_map/ppermute | solution.py:19
  77.2 7.1 collective-permute-start.15
  86.7 7.0 collective-permute-start.17
  90.6 7.5 collective-permute-start.16
  184.0 6.2 collective-permute-start.19
  190.2 6.2 collective-permute-start.20
  198.2 6.5 collective-permute-start.21
  204.8 7.0 collective-permute-start.22
  211.8 6.3 collective-permute-start.23
  294.8 5.9 collective-permute-start.25
  296.1 5.9 collective-permute-start.24
  305.0 6.5 collective-permute-start.26
  307.8 5.6 collective-permute-start.27
  316.6 6.8 collective-permute-start.29
  319.3 8.2 %collective-permute-start.28 = (f32[2,1,66,130]{3,2,1,0:T(8,128)S(1)}, f32[2,1,66,130]{3,2,1,0:T(8,128)S(1)}, u32[]{:S(2)}, u32[]{:S(2)}) collective-permute-start(f32[2,1,66,130]{3,2,1,0:T(8,128)S(1)} %get-tuple-element.104), channel_id=1, source_target_pairs={{1,0},{2,1},{3,2},{5,4},{6,5},{7,6},{9,8},{10,9},{11,10},{13,12},{... | collective-permute-start | bytes 205928 | tf_op jit(solution)/shard_map/ppermute | solution.py:22
  413.5 6.2 collective-permute-start.31
  419.7 6.2 collective-permute-start.32
  427.7 6.7 collective-permute-start.33
  434.4 6.5 collective-permute-start.34
  441.0 6.2 collective-permute-start.35
  447.6 5.9 collective-permute-start.37
  448.9 5.9 collective-permute-start.36
  458.0 7.6 collective-permute-start.38
  461.8 5.6 collective-permute-start.39
  470.6 7.9 collective-permute-start.41
  474.4 8.5 %collective-permute-start.40 = (f32[2,1,66,130]{3,2,1,0:T(8,128)S(1)}, f32[2,1,66,130]{3,2,1,0:T(8,128)S(1)}, u32[]{:S(2)}, u32[]{:S(2)}) collective-permute-start(f32[2,1,66,130]{3,2,1,0:T(8,128)S(1)} %get-tuple-element.102), channel_id=1, source_target_pairs={{1,0},{2,1},{3,2},{5,4},{6,5},{7,6},{9,8},{10,9},{11,10},{13,12},{... | collective-permute-start | bytes 205928 | tf_op jit(solution)/shard_map/ppermute | solution.py:22
  570.7 6.2 collective-permute-start.43
  576.9 6.2 collective-permute-start.44
  584.9 6.7 collective-permute-start.45
  591.6 6.5 collective-permute-start.46
  598.1 6.2 collective-permute-start.47
  682.1 5.9 collective-permute-start.49
  683.4 5.9 collective-permute-start.48
  691.8 7.1 collective-permute-start.50
  704.1 8.1 collective-permute-start.52
  (200 other events, 1553.7 us)
where the time goes:
time: 816 us; the launch traced here: 812 us
  blocking collectives  468 us (57%)
  starting transfers between devices  140 us (17%)
  waiting for transfers between devices  104 us (13%)
  local copies, waits for them, and re-layouts  47.8 us (6%)
  other arithmetic  38.1 us (5%)
  between operations  13.6 us (2%)
    psum x4, blocking collectives, norm_total(): return lax.psum(jnp.sum(residual * precond), ('gx', 'gy', 'gz'))  302 us
    psum x2, blocking collectives, curvature_total(): return lax.psum(jnp.sum(direction * image), ('gx', 'gy', 'gz'))  148 us
    ppermute x24, waiting for transfers between devices, from_behind(): return lax.ppermute(array, axis, pairs)  72.1 us
    ppermute x24, starting transfers between devices, from_behind(): return lax.ppermute(array, axis, pairs)  59.3 us
    ppermute x15, starting transfers between devices, with_halo(): lax.ppermute(lax.slice_in_dim(block, block.shape[dim] - width, None, axis...  50.5 us
    ppermute x15, starting transfers between devices, with_halo(): lax.ppermute(lax.slice_in_dim(block, 0, width, axis=dim), axis, backward)  30 us
    ppermute x15, waiting for transfers between devices, with_halo(): lax.ppermute(lax.slice_in_dim(block, 0, width, axis=dim), axis, backward)  18.5 us
    psum x1, blocking collectives, local(): hessian_action = lax.psum(local_terms, 'gz')  18.1 us
  transfers between devices with their start and end apart: 54, of which 34 were waited for; matrix products, arithmetic and copies ran while one was open for 3% of the time, Pallas kernels for 0%

commit v1 on v0

v1 whole, which is shorter than its diff:
```python
import functools

import jax
import jax.numpy as jnp
from jax import lax
from jax.experimental import pallas as pl
from jax.experimental.pallas import tpu as pltpu
from jax.sharding import PartitionSpec as P

TILE = 16
VERTICAL = 8.0
STRETCH = 4.0
NONE = 1000.0
MESH = pl.DeviceIdType.MESH
F32 = jnp.float32
NZ = 32
ROWS = 16
LANES = 128
UNROLL = 4


def blocked_loop(steps, body, carry):
    def chunk(index, state):
        for inner in range(UNROLL):
            state = body(index * UNROLL + inner, state)
        return state

    return lax.fori_loop(0, steps // UNROLL, chunk, carry)


def kernel(
    sizes,
    vel, visc, binv, coup, fric, fstep, misfit, ice, bed,
    inc, adj, hess,
    V, B, L, vbs, vbp, WU, WE, WW, WN, WS, D0, D1,
    Z0, ZA, S0, SA, ZB, SB,
    xs0, xr0, ps0, pr0, xs1, xr1, ps1, pr1, xs2, xr2, ps2, pr2, xs3, xr3, ps3, pr3,
    rt, ra, rb,
    loc_sem, in_send, in_recv, halo_send, halo_recv, red_send, red_recv_a, red_recv_b,
    out_send, out_recv,
):
    ngx, ngy, ngz = sizes
    gx, gy, gz = lax.axis_index("gx"), lax.axis_index("gy"), lax.axis_index("gz")
    depth = NZ // ngz
    odd = gx % 2

    def piece_of(q):
        return q + odd * (ngz - 1 - 2 * q)

    piece = piece_of(gz)
    total_pieces = ngx * ngz
    spot = gx * ngz + piece

    def holder(index):
        block = index // ngz
        part = index % ngz
        return (block, gy, part + (block % 2) * (ngz - 1 - 2 * part))

    x_low = holder((spot + total_pieces - 1) % total_pieces)
    x_high = holder((spot + 1) % total_pieces)
    y_low = (gx, (gy + ngy - 1) % ngy, gz)
    y_high = (gx, (gy + 1) % ngy, gz)
    peers = [(gx, gy, (gz + o) % ngz) for o in range(1, ngz)]
    half = ngz // 2
    na, nb = ngx * 2, ngy * half
    ma, mb = gx * 2 + gz % 2, gy * half + gz // 2

    def member_a(o):
        m = (ma + o) % na
        return (m // 2, gy, (gz // 2) * 2 + m % 2)

    def member_b(o):
        m = (mb + o) % nb
        return (gx, m // half, (m % half) * 2 + gz % 2)

    group_a = [member_a(o) for o in range(1, na)]
    group_b = [member_b(o) for o in range(1, nb)]

    barrier = pltpu.get_barrier_semaphore()
    partners = [x_low, x_high, y_low, y_high] + peers + group_a + group_b
    for partner in partners:
        pl.semaphore_signal(barrier, inc=1, device_id=partner, device_id_type=MESH)

    base = gz * depth
    bedf = bed[...]
    vb0 = jnp.zeros(bedf.shape, F32)
    vb1 = jnp.zeros(bedf.shape, F32)
    for k in range(depth):
        at = bedf == base + k
        vb0 = jnp.where(at, vel[0, k], vb0)
        vb1 = jnp.where(at, vel[1, k], vb1)
    vbs[0] = vb0
    vbs[1] = vb1

    pl.semaphore_wait(barrier, len(partners))

    here = pl.multiple_of(piece * ROWS, ROWS)
    layers = pl.ds(base, depth)

    def moves(part, o):
        rows = pl.ds(pl.multiple_of(part * ROWS, ROWS), ROWS)
        return [
            (visc.at[:, rows, :], V.at[layers]),
            (binv.at[:, :, rows, :], B.at[:, layers]),
            (coup.at[:, rows, :], L.at[layers]),
            (vbs.at[:, rows, :], vbp.at[o]),
        ]

    locals_in = []
    for a, (src, dst) in enumerate(moves(piece, 0)):
        copy = pltpu.make_async_copy(src, dst, loc_sem.at[a])
        copy.start()
        locals_in.append(copy)
    incoming = [[], [], [], []]
    per_peer = [moves(piece_of((gz + o) % ngz), o) for o in range(1, ngz)]
    for a in range(4):
        for o in range(1, ngz):
            src, dst = per_peer[o - 1][a]
            copy = pltpu.make_async_remote_copy(
                src_ref=src, dst_ref=dst,
                send_sem=in_send.at[a, o], recv_sem=in_recv.at[a, o],
                device_id=peers[o - 1], device_id_type=MESH,
            )
            copy.start()
            incoming[a].append(copy)

    row = lax.broadcasted_iota(jnp.int32, (ROWS, LANES), 0)
    lane = lax.broadcasted_iota(jnp.int32, (ROWS, LANES), 1)
    column = jnp.zeros((ROWS, LANES), F32)
    for j in range(LANES // TILE):
        flag = ice[piece, j].astype(F32)
        column = jnp.where(lane // TILE == j, flag, column)
    has_ice = column > 0.5
    my_rows = pl.ds(here, ROWS)
    kbed = jnp.where(has_ice, bed[my_rows, :].astype(F32), NONE)
    friction = fric[my_rows, :]
    load = misfit[my_rows, :] * column

    for field in (Z0, ZA, S0, SA, ZB, SB):
        for c in range(2):
            field[c, 0] = jnp.zeros((ROWS, LANES), F32)
            field[c, NZ + 1] = jnp.zeros((ROWS, LANES), F32)
    for ps in (ps0, ps3):
        ps[...] = jnp.zeros(ps.shape, F32)

    def pack_lane(packed, value, j):
        low, high = packed
        low = jnp.where(lane == j, pltpu.roll(value, j, 1), low)
        high = jnp.where(lane == j, pltpu.roll(value, (j + 1) % LANES, 1), high)
        return low, high

    def pack_rows(xs, value, j):
        xs[0, pl.ds(j, 1), :] = value[0:1, :]
        xs[1, pl.ds(j, 1), :] = value[ROWS - 1 : ROWS, :]

    def send_halo(index, xs, xr, ps, pr):
        copies = []
        for side, (src, dst, device) in enumerate(
            [
                (ps.at[0], pr.at[1], y_low),
                (ps.at[1], pr.at[0], y_high),
                (xs.at[0], xr.at[1], x_low),
                (xs.at[1], xr.at[0], x_high),
            ]
        ):
            copy = pltpu.make_async_remote_copy(
                src_ref=src, dst_ref=dst,
                send_sem=halo_send.at[index, side], recv_sem=halo_recv.at[index, side],
                device_id=device, device_id_type=MESH,
            )
            copy.start()
            copies.append(copy)
        return copies

    def beside(value, xr, xj, left, right, lj):
        east = jnp.where(row == ROWS - 1, xr[1, pl.ds(xj, 1), :], pltpu.roll(value, ROWS - 1, 0))
        west = jnp.where(row == 0, xr[0, pl.ds(xj, 1), :], pltpu.roll(value, 1, 0))
        north = jnp.where(
            lane == LANES - 1, pltpu.roll(right, LANES - 1 - lj, 1), pltpu.roll(value, LANES - 1, 1)
        )
        south = jnp.where(
            lane == 0, pltpu.roll(left, (LANES - lj) % LANES, 1), pltpu.roll(value, 1, 1)
        )
        return east, west, north, south

    locals_in[0].wait()
    for copy in incoming[0]:
        copy.wait_recv()

    def pack_viscosity(k, packed):
        value = V[k]
        pack_rows(xs0, value, k)
        return pack_lane(packed, value, k)

    blank = jnp.zeros((ROWS, LANES), F32)
    packed = blocked_loop(NZ, pack_viscosity, (blank, blank))
    pack_rows(xs0, kbed, NZ)
    low, high = pack_lane(packed, kbed, NZ)
    ps0[0] = low
    ps0[1] = high
    halo0 = send_halo(0, xs0, xr0, ps0, pr0)

    for copy in halo0:
        copy.wait_recv()
    left, right = pr0[0], pr0[1]
    bed_e, bed_w, bed_n, bed_s = beside(kbed, xr0, NZ, left, right, NZ)
    bed_e = jnp.where((row == ROWS - 1) & (spot == total_pieces - 1), NONE, bed_e)
    bed_w = jnp.where((row == 0) & (spot == 0), NONE, bed_w)
    bed_n = jnp.where((lane == LANES - 1) & (gy == ngy - 1), NONE, bed_n)
    bed_s = jnp.where((lane == 0) & (gy == 0), NONE, bed_s)

    def layer_weights(k, carry):
        below_v, below_a = carry
        level = jnp.full((ROWS, LANES), k, jnp.int32).astype(F32)
        value = V[k]
        act = jnp.where(level >= kbed, 1.0, 0.0)
        bedflag = jnp.where(level == kbed, 1.0, 0.0)
        east, west, north, south = beside(value, xr0, k, left, right, k)
        half_act = 0.5 * act
        down = (VERTICAL * (value + below_v)) * (half_act * below_a)
        we = (value + east) * jnp.where(level >= bed_e, half_act, 0.0)
        ww = (value + west) * jnp.where(level >= bed_w, half_act, 0.0)
        wn = (value + north) * jnp.where(level >= bed_n, half_act, 0.0)
        ws = (value + south) * jnp.where(level >= bed_s, half_act, 0.0)
        WU[k] = down
        WE[k] = we
        WW[k] = ww
        WN[k] = wn
        WS[k] = ws
        ew, ns = we + ww, wn + ws
        rest = friction * bedflag + (1.0 - act)
        D0[k] = down + STRETCH * ew + ns + rest
        D1[k] = down + ew + STRETCH * ns + rest
        return value, act

    blocked_loop(NZ, layer_weights, (blank, blank))
    WU[NZ] = blank

    for group, copy in zip(incoming[1:], locals_in[1:]):
        copy.wait()
        for remote in group:
            remote.wait_recv()
    speed0 = vbp[0, 0]
    speed1 = vbp[0, 1]
    for o in range(1, ngz):
        speed0 = speed0 + vbp[o, 0]
        speed1 = speed1 + vbp[o, 1]
    speed0 = jnp.where(has_ice, speed0, 0.0)
    speed1 = jnp.where(has_ice, speed1, 0.0)
    drive = friction * fstep[my_rows, :]
    push0, push1 = drive * speed0, drive * speed1

    def apply_inverse(k, first, second):
        b0, b1, b2 = B[0, k], B[1, k], B[2, k]
        return b0 * first + b1 * second, b1 * first + b2 * second

    def rise(k, first, second, state, out):
        y0, y1, total = state
        link = L[k]
        t0 = first + link * y0
        t1 = second + link * y1
        y0, y1 = apply_inverse(k, t0, t1)
        out[0, k + 1] = y0
        out[1, k + 1] = y1
        return y0, y1, total + (t0 * y0 + t1 * y1)

    def first_rise(k, state):
        level = jnp.full((ROWS, LANES), k, jnp.int32).astype(F32)
        act = jnp.where(level >= kbed, 1.0, 0.0)
        beneath = jnp.where(level - 1.0 >= kbed, 1.0, 0.0)
        rest = 1.0 - act
        B[0, k] = act * B[0, k] + rest
        B[1, k] = act * B[1, k]
        B[2, k] = act * B[2, k] + rest
        L[k] = L[k] * act * beneath
        at = level == kbed
        first = jnp.where(at, push0, 0.0)
        second = jnp.where(at, push1, 0.0)
        above = WU[k + 1]
        D0[k] = D0[k] + above
        D1[k] = D1[k] + above
        return rise(k, first, second, state, Z0)

    state = blocked_loop(NZ, first_rise, (blank, blank, blank))
    rz0 = state[2]

    def fall(k, g0, g1, field):
        add0, add1 = apply_inverse(k, g0, g1)
        z0 = field[0, k + 1] + add0
        z1 = field[1, k + 1] + add1
        field[0, k + 1] = z0
        field[1, k + 1] = z1
        link = L[k]
        return z0, z1, link * z0, link * z1

    def fall_bare(k, g0, g1, field):
        z0, z1 = apply_inverse(k, g0, g1)
        field[0, k + 1] = z0
        field[1, k + 1] = z1
        link = L[k]
        return z0, z1, link * z0, link * z1

    seed_a0, seed_a1 = load * Z0[0, NZ], load * Z0[1, NZ]

    def fall_first(i, carry):
        k = NZ - 1 - i
        g0, g1, a0, a1, low, high = carry
        z0, z1, g0, g1 = fall(k, g0, g1, Z0)
        y0, y1, a0, a1 = fall_bare(k, a0, a1, ZA)
        packed = (low, high)
        for n, value in enumerate((z0, z1, y0, y1)):
            pack_rows(xs1, value, k + NZ * n)
            packed = pack_lane(packed, value, k + NZ * n)
        return (g0, g1, a0, a1) + packed

    carry = blocked_loop(NZ, fall_first, (blank, blank, seed_a0, seed_a1, blank, blank))
    ps1[0] = carry[4]
    ps1[1] = carry[5]
    halo1 = send_halo(1, xs1, xr1, ps1, pr1)
    raa = seed_a0 * ZA[0, NZ] + seed_a1 * ZA[1, NZ]

    def operate(k, weights, field, xr, xj, left, right, lj):
        up, down, we, ww, wn, ws, d0, d1 = weights
        result = []
        for c in range(2):
            value = field[c, k + 1]
            east, west, north, south = beside(
                value, xr, xj + c * NZ + k, left, right, lj + c * NZ + k
            )
            vertical = up * field[c, k + 2] + down * field[c, k]
            ew = we * east + ww * west
            ns = wn * north + ws * south
            if c == 0:
                result.append(d0 * value - vertical - STRETCH * ew - ns)
            else:
                result.append(d1 * value - vertical - ew - STRETCH * ns)
        return result

    def weights_of(k):
        return WU[k + 1], WU[k], WE[k], WW[k], WN[k], WS[k], D0[k], D1[k]

    def against(field, k, image, total):
        return total + (field[0, k + 1] * image[0] + field[1, k + 1] * image[1])

    for copy in halo1:
        copy.wait_recv()
    left1, right1 = pr1[0], pr1[1]

    def middle_rise(k, carry):
        pq0, paa, main, extra = carry
        weights = weights_of(k)
        w = operate(k, weights, Z0, xr1, 0, left1, right1, 0)
        wa = operate(k, weights, ZA, xr1, 2 * NZ, left1, right1, 2 * NZ)
        pq0 = against(Z0, k, w, pq0)
        paa = against(ZA, k, wa, paa)
        main = rise(k, w[0], w[1], main, S0)
        extra = rise(k, wa[0], wa[1], extra, SA)
        return pq0, paa, main, extra

    triple = (blank, blank, blank)
    pq0, paa, main, extra = blocked_loop(NZ, middle_rise, (blank, blank, triple, triple))
    g0, gaa = main[2], extra[2]
    seed_b0, seed_b1 = load * S0[0, NZ], load * S0[1, NZ]

    def fall_second(i, carry):
        k = NZ - 1 - i
        g0, g1, h0, h1, b0, b1, low1, high1, low2, high2 = carry
        z0, z1, g0, g1 = fall(k, g0, g1, S0)
        a0, a1, h0, h1 = fall(k, h0, h1, SA)
        y0, y1, b0, b1 = fall_bare(k, b0, b1, ZB)
        packed = (low1, high1)
        for n, value in enumerate((y0, y1, z0, z1)):
            pack_rows(xs2, value, k + NZ * n)
            packed = pack_lane(packed, value, k + NZ * n)
        other = (low2, high2)
        for n, value in enumerate((a0, a1)):
            pack_rows(xs2, value, k + NZ * (n + 4))
            other = pack_lane(other, value, k + NZ * n)
        return (g0, g1, h0, h1, b0, b1) + packed + other

    carry = blocked_loop(
        NZ, fall_second, (blank, blank, blank, blank, seed_b0, seed_b1, blank, blank, blank, blank)
    )
    for n in range(2):
        ps2[0, ROWS * n : ROWS * (n + 1), :] = carry[6 + 2 * n]
        ps2[1, ROWS * n : ROWS * (n + 1), :] = carry[7 + 2 * n]
    halo2 = send_halo(2, xs2, xr2, ps2, pr2)
    rab = seed_a0 * ZB[0, NZ] + seed_a1 * ZB[1, NZ]
    rbb = seed_b0 * ZB[0, NZ] + seed_b1 * ZB[1, NZ]

    for copy in halo2:
        copy.wait_recv()
    left2, right2 = pr2[0, :ROWS, :], pr2[1, :ROWS, :]
    left3, right3 = pr2[0, ROWS:, :], pr2[1, ROWS:, :]

    def last_rise(k, carry):
        pab, pbb, gab, main = carry
        w = operate(k, weights_of(k), ZB, xr2, 0, left2, right2, 0)
        pab = against(ZA, k, w, pab)
        pbb = against(ZB, k, w, pbb)
        gab = against(SA, k, w, gab)
        main = rise(k, w[0], w[1], main, SB)
        return pab, pbb, gab, main

    pab, pbb, gab, main = blocked_loop(NZ, last_rise, (blank, blank, blank, triple))
    gbb = main[2]

    def fall_third(i, carry):
        k = NZ - 1 - i
        g0, g1, low, high = carry
        z0, z1, g0, g1 = fall(k, g0, g1, SB)
        packed = (low, high)
        for n, value in enumerate((z0, z1)):
            pack_rows(xs3, value, k + NZ * n)
            packed = pack_lane(packed, value, k + NZ * n)
        return (g0, g1) + packed

    carry = blocked_loop(NZ, fall_third, (blank, blank, blank, blank))
    ps3[0] = carry[2]
    ps3[1] = carry[3]
    halo3 = send_halo(3, xs3, xr3, ps3, pr3)

    def early_energy(k, carry):
        d0, daa = carry
        weights = weights_of(k)
        w = operate(k, weights, S0, xr2, 2 * NZ, left2, right2, 2 * NZ)
        wa = operate(k, weights, SA, xr2, 4 * NZ, left3, right3, 0)
        return against(S0, k, w, d0), against(SA, k, wa, daa)

    d0, daa = blocked_loop(NZ, early_energy, (blank, blank))

    for copy in halo3:
        copy.wait_recv()
    left4, right4 = pr3[0], pr3[1]

    def late_energy(k, carry):
        dab, dbb = carry
        w = operate(k, weights_of(k), SB, xr3, 0, left4, right4, 0)
        return against(SA, k, w, dab), against(SB, k, w, dbb)

    dab, dbb = blocked_loop(NZ, late_energy, (blank, blank))

    sums = [rz0, pq0, g0, d0, raa, rab, rbb, paa, pab, pbb, gaa, gab, gbb, daa, dab, dbb]
    for n, value in enumerate(sums):
        rt[0, n : n + 1, :] = jnp.sum(value, axis=0, keepdims=True)
    reductions = []
    for turn, (group, received, sem) in enumerate(((group_a, ra, red_recv_a), (group_b, rb, red_recv_b))):
        copies = []
        for o, device in enumerate(group):
            copy = pltpu.make_async_remote_copy(
                src_ref=rt.at[turn], dst_ref=received.at[o],
                send_sem=red_send.at[turn, o], recv_sem=sem.at[o],
                device_id=device, device_id_type=MESH,
            )
            copy.start()
            copies.append(copy)
        total = rt[turn]
        for o, copy in enumerate(copies):
            copy.wait_recv()
            total = total + received[o]
        if turn == 0:
            rt[1] = total
        reductions += copies
    totals = jnp.broadcast_to(jnp.sum(total, axis=1, keepdims=True), (ROWS, LANES))
    (rz0, pq0, g0, d0, raa, rab, rbb, paa, pab, pbb, gaa, gab, gbb, daa, dab, dbb) = [
        totals[n : n + 1, :] for n in range(16)
    ]

    def combination(rz, pq, g, d):
        step = rz / pq
        renewed = step * step * g - rz
        grow = 1.0 + renewed / rz
        energy = grow * grow * pq - 2.0 * grow * step * g + step * step * d
        second = renewed / energy
        return step + second * grow, -(second * step)

    c0, c1 = combination(rz0, pq0, g0, d0)

    def form(aa, ab, bb):
        return c0 * c0 * aa + 2.0 * (c0 * c1) * ab + c1 * c1 * bb

    e0, e1 = combination(form(raa, rab, rbb), form(paa, pab, pbb), form(gaa, gab, gbb), form(daa, dab, dbb))
    f_za, f_zb, f_sa, f_sb = e0 * c0, e0 * c1, e1 * c0, e1 * c1

    def results(k, carry):
        level = jnp.full((ROWS, LANES), k, jnp.int32).astype(F32)
        at = level == kbed
        out = []
        for c in range(2):
            Z0[c, k + 1] = c0 * Z0[c, k + 1] + c1 * S0[c, k + 1]
            value = (f_za * ZA[c, k + 1] + f_zb * ZB[c, k + 1]) + (f_sa * SA[c, k + 1] + f_sb * SB[c, k + 1])
            ZA[c, k + 1] = value
            out.append(jnp.where(at, value, carry[c]))
        return tuple(out)

    basal = blocked_loop(NZ, results, (blank, blank))
    action = friction * (speed0 * basal[0] + speed1 * basal[1])
    hess[my_rows, :] = action
    vbs[0, my_rows, :] = action

    finals = []
    rest = []
    back = (inc.at[:, :, my_rows, :], adj.at[:, :, my_rows, :], hess.at[my_rows, :])
    for n, field in enumerate((Z0, ZA)):
        copy = pltpu.make_async_copy(field.at[:, pl.ds(1 + base, depth)], back[n], loc_sem.at[n])
        copy.start()
        finals.append(copy)
    for o in range(1, ngz):
        theirs = pl.ds(1 + ((gz + o) % ngz) * depth, depth)
        for n, src in enumerate((Z0.at[:, theirs], ZA.at[:, theirs], vbs.at[0, my_rows, :])):
            copy = pltpu.make_async_remote_copy(
                src_ref=src, dst_ref=back[n],
                send_sem=out_send.at[n, o], recv_sem=out_recv.at[n, o],
                device_id=peers[o - 1], device_id_type=MESH,
            )
            copy.start()
            rest.append(copy)
    for copy in finals:
        copy.wait()
    for copy in rest:
        copy.wait()
    for group in incoming:
        for copy in group:
            copy.wait_send()
    for copy in halo0 + halo1 + halo2 + halo3 + reductions:
        copy.wait_send()


def local(sizes, *args):
    ngx, ngy, ngz = sizes
    field = pltpu.VMEM((NZ, ROWS, LANES), F32)
    state = pltpu.VMEM((2, NZ + 2, ROWS, LANES), F32)
    depth, rows, lanes = args[1].shape
    dma = pltpu.SemaphoreType.DMA

    def halo(length, packs):
        return [pltpu.VMEM((2, length, LANES), F32)] * 2 + [pltpu.VMEM((2, packs * ROWS, LANES), F32)] * 2

    na, nb = ngx * 2, ngy * (ngz // 2)
    scratch = (
        [field, pltpu.VMEM((3, NZ, ROWS, LANES), F32), field]
        + [pltpu.VMEM((2, rows, lanes), F32), pltpu.VMEM((ngz, 2, ROWS, LANES), F32)]
        + [pltpu.VMEM((NZ + 1, ROWS, LANES), F32)]
        + [field] * 6
        + [state] * 6
        + halo(NZ + 8, 1) + halo(4 * NZ, 1) + halo(6 * NZ, 2) + halo(2 * NZ, 1)
        + [pltpu.VMEM((2, ROWS, LANES), F32)]
        + [pltpu.VMEM((na - 1, ROWS, LANES), F32), pltpu.VMEM((nb - 1, ROWS, LANES), F32)]
        + [dma((4,)), dma((4, ngz)), dma((4, ngz)), dma((4, 4)), dma((4, 4))]
        + [dma((2, max(na, nb))), dma((na,)), dma((nb,)), dma((3, ngz)), dma((3, ngz))]
    )
    vmem = pl.BlockSpec(memory_space=pltpu.VMEM)
    hbm = pl.BlockSpec(memory_space=pl.ANY)
    smem = pl.BlockSpec(memory_space=pltpu.SMEM)
    return pl.pallas_call(
        functools.partial(kernel, sizes),
        out_shape=(
            jax.ShapeDtypeStruct((2, depth, rows, lanes), F32),
            jax.ShapeDtypeStruct((2, depth, rows, lanes), F32),
            jax.ShapeDtypeStruct((rows, lanes), F32),
        ),
        in_specs=[vmem, hbm, hbm, hbm, vmem, vmem, vmem, smem, vmem],
        out_specs=(hbm, hbm, vmem),
        scratch_shapes=scratch,
        compiler_params=pltpu.CompilerParams(
            collective_id=0, has_side_effects=True, vmem_limit_bytes=40 * 1024 * 1024
        ),
    )(*args)


def solution(mesh):
    sizes = (mesh.shape["gx"], mesh.shape["gy"], mesh.shape["gz"])
    wide, cell, flat = P(None, "gz", "gx", "gy"), P("gz", "gx", "gy"), P("gx", "gy")
    return jax.shard_map(
        functools.partial(local, sizes),
        mesh=mesh,
        in_specs=(wide, cell, wide, cell, flat, flat, flat, flat, flat),
        out_specs=(wide, wide, flat),
        check_vma=False,
    )
```

time: 816 us -> 88.2 us (0.11)
  the two profiles are of different devices: /device:TPU:2 before, /device:TPU:1 now
where the time goes in v1:
time: 88.2 us; the launch traced here: 87.7 us
  Pallas kernels  77.1 us (87%)
  local copies, waits for them, and re-layouts  9.98 us (11%)
    pallas_call x1, Pallas kernels, local(): pl.pallas_call(functools.partial(kernel, sizes), out_shape=(jax.ShapeDtyp...  77.1 us
    unnamed x21, local copies, waits for them, and re-layouts  9.98 us

profile of v1, /device:TPU:1, one launch (start us, length us, event | category | flops | bytes accessed | tf_op | source)
XLA Modules:
  0.0 87.7 jit_solution(14211042952535296188)
XLA Ops:
  0.6 0.0 copy-start
  0.6 1.1 %copy-done = f32[3,8,64,128]{3,2,1,0:T(8,128)S(1)} copy-done((f32[3,8,64,128]{3,2,1,0:T(8,128)S(1)}, f32[3,8,64,128]{3,2,1,0:T(8,128)}, u32[]{:S(2)}) %copy-start) | copy-done | bytes 786456
  1.8 0.0 copy-start.1
  1.8 1.0 %copy-done.1 = f32[2,8,64,128]{3,2,1,0:T(8,128)S(1)} copy-done((f32[2,8,64,128]{3,2,1,0:T(8,128)S(1)}, f32[2,8,64,128]{3,2,1,0:T(8,128)}, u32[]{:S(2)}) %copy-start.1) | copy-done | bytes 524312
  2.8 0.0 copy-start.2
  2.8 0.9 %copy-done.2 = f32[8,64,128]{2,1,0:T(8,128)S(1)} copy-done((f32[8,64,128]{2,1,0:T(8,128)S(1)}, f32[8,64,128]{2,1,0:T(8,128)}, u32[]{:S(2)}) %copy-start.2) | copy-done | bytes 262168
  3.8 0.0 copy-start.3
  3.8 0.9 %copy-done.3 = f32[8,64,128]{2,1,0:T(8,128)S(1)} copy-done((f32[8,64,128]{2,1,0:T(8,128)S(1)}, f32[8,64,128]{2,1,0:T(8,128)}, u32[]{:S(2)}) %copy-start.3) | copy-done | bytes 262168
  4.7 0.0 copy-start.4
  4.7 0.8 copy-done.4
  5.5 0.0 copy-start.5
  5.5 0.8 copy-done.5
  6.2 0.0 copy-start.6
  6.2 0.8 copy-done.6
  7.0 0.0 copy-start.7
  7.0 0.8 copy-done.7
  7.7 0.0 copy-start.8
  7.7 0.7 copy-done.8
  8.4 77.1 %shard_map.112 = (f32[2,8,64,128]{3,2,1,0:T(8,128)S(1)}, f32[2,8,64,128]{3,2,1,0:T(8,128)S(1)}, f32[64,128]{1,0:T(8,128)S(1)}) custom-call(f32[2,8,64,128]{3,2,1,0:T(8,128)S(1)} %copy-done.1, f32[8,64,128]{2,1,0:T(8,128)S(1)} %copy-done.2, f32[3,8,64,128]{3,2,1,0:T(8,128)S(1)} %copy-done, f32[8,64,128]{2,1,0:T(8,128)S(1)} %copy-done.3, ...), custom_call_target="tpu_custom_call" | custom-call | tf_op jit(solution)/shard_map/pallas_call | solution.py:555
  85.5 0.8 copy.15
  86.3 0.8 copy.16
  87.1 0.6 copy.17
Async XLA Ops:
  0.6 1.1 %copy-start = (f32[3,8,64,128]{3,2,1,0:T(8,128)S(1)}, f32[3,8,64,128]{3,2,1,0:T(8,128)}, u32[]{:S(2)}) copy-start(f32[3,8,64,128]{3,2,1,0:T(8,128)} %binv.1) | copy-start | bytes 2359300
  1.8 1.0 %copy-start.1 = (f32[2,8,64,128]{3,2,1,0:T(8,128)S(1)}, f32[2,8,64,128]{3,2,1,0:T(8,128)}, u32[]{:S(2)}) copy-start(f32[2,8,64,128]{3,2,1,0:T(8,128)} %vel.1) | copy-start | bytes 1572868
  2.8 0.9 %copy-start.2 = (f32[8,64,128]{2,1,0:T(8,128)S(1)}, f32[8,64,128]{2,1,0:T(8,128)}, u32[]{:S(2)}) copy-start(f32[8,64,128]{2,1,0:T(8,128)} %visc.1) | copy-start | bytes 786436
  3.8 0.9 %copy-start.3 = (f32[8,64,128]{2,1,0:T(8,128)S(1)}, f32[8,64,128]{2,1,0:T(8,128)}, u32[]{:S(2)}) copy-start(f32[8,64,128]{2,1,0:T(8,128)} %coup.1) | copy-start | bytes 786436
  4.7 0.8 copy-start.4
  5.5 0.8 copy-start.5
  6.2 0.8 copy-start.6
  7.0 0.8 copy-start.7
  7.7 0.7 copy-start.8

commit v2 on v1

--- a/solution.py
+++ b/solution.py
@@ -16,7 +16,7 @@
 NZ = 32
 ROWS = 16
 LANES = 128
-UNROLL = 4
+UNROLL = 8
 
 
 def blocked_loop(steps, body, carry):
@@ -30,13 +30,14 @@
 
 def kernel(
     sizes,
-    vel, visc, binv, coup, fric, fstep, misfit, ice, bed,
+    vel_in, visc, binv, coup, fric_in, fstep_in, misfit_in, ice, bed_in,
     inc, adj, hess,
+    vel, bed, fric, fstep, misfit,
     V, B, L, vbs, vbp, WU, WE, WW, WN, WS, D0, D1,
     Z0, ZA, S0, SA, ZB, SB,
     xs0, xr0, ps0, pr0, xs1, xr1, ps1, pr1, xs2, xr2, ps2, pr2, xs3, xr3, ps3, pr3,
-    rt, ra, rb,
-    loc_sem, in_send, in_recv, halo_send, halo_recv, red_send, red_recv_a, red_recv_b,
+    stack, rt, ra, rb,
+    load_sem, loc_sem, in_send, in_recv, halo_send, halo_recv, red_send, red_recv_a, red_recv_b,
     out_send, out_recv,
 ):
     ngx, ngy, ngz = sizes
@@ -61,20 +62,36 @@
     y_low = (gx, (gy + ngy - 1) % ngy, gz)
     y_high = (gx, (gy + 1) % ngy, gz)
     peers = [(gx, gy, (gz + o) % ngz) for o in range(1, ngz)]
-    half = ngz // 2
-    na, nb = ngx * 2, ngy * half
-    ma, mb = gx * 2 + gz % 2, gy * half + gz // 2
+    na, nb = ngx * 2, (ngy // 2) * ngz
+    core = gy % 2
+    ma, mb = gx * 2 + core, (gy // 2) * ngz + gz
 
     def member_a(o):
         m = (ma + o) % na
-        return (m // 2, gy, (gz // 2) * 2 + m % 2)
+        return (m // 2, (gy // 2) * 2 + m % 2, gz)
 
     def member_b(o):
         m = (mb + o) % nb
-        return (gx, m // half, (m % half) * 2 + gz % 2)
+        return (gx, (m // ngz) * 2 + core, m % ngz)
 
     group_a = [member_a(o) for o in range(1, na)]
     group_b = [member_b(o) for o in range(1, nb)]
+
+    here = pl.multiple_of(piece * ROWS, ROWS)
+    my_rows = pl.ds(here, ROWS)
+    loads = []
+    for n, (src, dst) in enumerate(
+        [
+            (bed_in, bed),
+            (vel_in, vel),
+            (fric_in.at[my_rows, :], fric),
+            (fstep_in.at[my_rows, :], fstep),
+            (misfit_in.at[my_rows, :], misfit),
+        ]
+    ):
+        copy = pltpu.make_async_copy(src, dst, load_sem.at[n])
+        copy.start()
+        loads.append(copy)
 
     barrier = pltpu.get_barrier_semaphore()
     partners = [x_low, x_high, y_low, y_high] + peers + group_a + group_b
@@ -82,6 +99,8 @@
         pl.semaphore_signal(barrier, inc=1, device_id=partner, device_id_type=MESH)
 
     base = gz * depth
+    for copy in loads:
+        copy.wait()
     bedf = bed[...]
     vb0 = jnp.zeros(bedf.shape, F32)
     vb1 = jnp.zeros(bedf.shape, F32)
@@ -94,7 +113,6 @@
 
     pl.semaphore_wait(barrier, len(partners))
 
-    here = pl.multiple_of(piece * ROWS, ROWS)
     layers = pl.ds(base, depth)
 
     def moves(part, o):
@@ -131,10 +149,9 @@
         flag = ice[piece, j].astype(F32)
         column = jnp.where(lane // TILE == j, flag, column)
     has_ice = column > 0.5
-    my_rows = pl.ds(here, ROWS)
     kbed = jnp.where(has_ice, bed[my_rows, :].astype(F32), NONE)
-    friction = fric[my_rows, :]
-    load = misfit[my_rows, :] * column
+    friction = fric[...]
+    load = misfit[...] * column
 
     for field in (Z0, ZA, S0, SA, ZB, SB):
         for c in range(2):
@@ -247,7 +264,7 @@
         speed1 = speed1 + vbp[o, 1]
     speed0 = jnp.where(has_ice, speed0, 0.0)
     speed1 = jnp.where(has_ice, speed1, 0.0)
-    drive = friction * fstep[my_rows, :]
+    drive = friction * fstep[...]
     push0, push1 = drive * speed0, drive * speed1
 
     def apply_inverse(k, first, second):
@@ -429,6 +446,42 @@
 
     d0, daa = blocked_loop(NZ, early_energy, (blank, blank))
 
+    stages = ((group_a, ra, red_recv_a), (group_b, rb, red_recv_b))
+
+    def gather_sums(values, turn):
+        for n, value in enumerate(values):
+            stack[turn, n : n + 1, :] = jnp.sum(value, axis=0, keepdims=True)
+        each = jnp.sum(stack[turn], axis=1, keepdims=True)
+        return jnp.sum(jnp.where(lane == row, each, 0.0), axis=0, keepdims=True)
+
+    def send_sum(turn, stage, value):
+        rt[turn, stage] = value
+        group, received, sem = stages[stage]
+        copies = []
+        for o, device in enumerate(group):
+            copy = pltpu.make_async_remote_copy(
+                src_ref=rt.at[turn, stage], dst_ref=received.at[turn, o],
+                send_sem=red_send.at[turn, stage, o], recv_sem=sem.at[turn, o],
+                device_id=device, device_id_type=MESH,
+            )
+            copy.start()
+            copies.append(copy)
+        return copies
+
+    def finish_sum(turn, stage, copies):
+        for copy in copies:
+            copy.wait_recv()
+        received = stages[stage][1]
+        return rt[turn, stage] + jnp.sum(received[turn], axis=0)
+
+    def spread(total, count):
+        each = jnp.sum(jnp.where(lane == row, total, 0.0), axis=1, keepdims=True)
+        each = jnp.broadcast_to(each, (ROWS, LANES))
+        return [each[n : n + 1, :] for n in range(count)]
+
+    stack[...] = jnp.zeros(stack.shape, F32)
+    first_a = send_sum(0, 0, gather_sums([rz0, pq0, g0, d0], 0))
+
     for copy in halo3:
         copy.wait_recv()
     left4, right4 = pr3[0], pr3[1]
@@ -440,31 +493,13 @@
 
     dab, dbb = blocked_loop(NZ, late_energy, (blank, blank))
 
-    sums = [rz0, pq0, g0, d0, raa, rab, rbb, paa, pab, pbb, gaa, gab, gbb, daa, dab, dbb]
-    for n, value in enumerate(sums):
-        rt[0, n : n + 1, :] = jnp.sum(value, axis=0, keepdims=True)
-    reductions = []
-    for turn, (group, received, sem) in enumerate(((group_a, ra, red_recv_a), (group_b, rb, red_recv_b))):
-        copies = []
-        for o, device in enumerate(group):
-            copy = pltpu.make_async_remote_copy(
-                src_ref=rt.at[turn], dst_ref=received.at[o],
-                send_sem=red_send.at[turn, o], recv_sem=sem.at[o],
-                device_id=device, device_id_type=MESH,
-            )
-            copy.start()
-            copies.append(copy)
-        total = rt[turn]
-        for o, copy in enumerate(copies):
-            copy.wait_recv()
-            total = total + received[o]
-        if turn == 0:
-            rt[1] = total
-        reductions += copies
-    totals = jnp.broadcast_to(jnp.sum(total, axis=1, keepdims=True), (ROWS, LANES))
-    (rz0, pq0, g0, d0, raa, rab, rbb, paa, pab, pbb, gaa, gab, gbb, daa, dab, dbb) = [
-        totals[n : n + 1, :] for n in range(16)
-    ]
+    second_a = send_sum(
+        1, 0, gather_sums([raa, rab, rbb, paa, pab, pbb, gaa, gab, gbb, daa, dab, dbb], 1)
+    )
+    first_b = send_sum(0, 1, finish_sum(0, 0, first_a))
+    second_b = send_sum(1, 1, finish_sum(1, 0, second_a))
+    reductions = first_a + second_a + first_b + second_b
+    rz0, pq0, g0, d0 = spread(finish_sum(0, 1, first_b), 4)
 
     def combination(rz, pq, g, d):
         step = rz / pq
@@ -476,45 +511,60 @@
 
     c0, c1 = combination(rz0, pq0, g0, d0)
 
+    def increments(k, carry):
+        for c in range(2):
+            Z0[c, k + 1] = c0 * Z0[c, k + 1] + c1 * S0[c, k + 1]
+        return carry
+
+    blocked_loop(NZ, increments, 0)
+    finals = []
+    rest = []
+    back = (inc.at[:, :, my_rows, :], adj.at[:, :, my_rows, :], hess.at[my_rows, :])
+
+    def give_back(n, field):
+        copy = pltpu.make_async_copy(field.at[:, pl.ds(1 + base, depth)], back[n], loc_sem.at[n])
+        copy.start()
+        finals.append(copy)
+        for o in range(1, ngz):
+            theirs = pl.ds(1 + ((gz + o) % ngz) * depth, depth)
+            send_back(n, o, field.at[:, theirs])
+
+    def send_back(n, o, src):
+        copy = pltpu.make_async_remote_copy(
+            src_ref=src, dst_ref=back[n],
+            send_sem=out_send.at[n, o], recv_sem=out_recv.at[n, o],
+            device_id=peers[o - 1], device_id_type=MESH,
+        )
+        copy.start()
+        rest.append(copy)
+
+    give_back(0, Z0)
+
+    raa, rab, rbb, paa, pab, pbb, gaa, gab, gbb, daa, dab, dbb = spread(finish_sum(1, 1, second_b), 12)
+
     def form(aa, ab, bb):
         return c0 * c0 * aa + 2.0 * (c0 * c1) * ab + c1 * c1 * bb
 
     e0, e1 = combination(form(raa, rab, rbb), form(paa, pab, pbb), form(gaa, gab, gbb), form(daa, dab, dbb))
     f_za, f_zb, f_sa, f_sb = e0 * c0, e0 * c1, e1 * c0, e1 * c1
 
-    def results(k, carry):
+    def adjoints(k, carry):
         level = jnp.full((ROWS, LANES), k, jnp.int32).astype(F32)
         at = level == kbed
         out = []
         for c in range(2):
-            Z0[c, k + 1] = c0 * Z0[c, k + 1] + c1 * S0[c, k + 1]
             value = (f_za * ZA[c, k + 1] + f_zb * ZB[c, k + 1]) + (f_sa * SA[c, k + 1] + f_sb * SB[c, k + 1])
             ZA[c, k + 1] = value
             out.append(jnp.where(at, value, carry[c]))
         return tuple(out)
 
-    basal = blocked_loop(NZ, results, (blank, blank))
+    basal = blocked_loop(NZ, adjoints, (blank, blank))
+    give_back(1, ZA)
     action = friction * (speed0 * basal[0] + speed1 * basal[1])
     hess[my_rows, :] = action
     vbs[0, my_rows, :] = action
-
-    finals = []
-    rest = []
-    back = (inc.at[:, :, my_rows, :], adj.at[:, :, my_rows, :], hess.at[my_rows, :])
-    for n, field in enumerate((Z0, ZA)):
-        copy = pltpu.make_async_copy(field.at[:, pl.ds(1 + base, depth)], back[n], loc_sem.at[n])
-        copy.start()
-        finals.append(copy)
     for o in range(1, ngz):
-        theirs = pl.ds(1 + ((gz + o) % ngz) * depth, depth)
-        for n, src in enumerate((Z0.at[:, theirs], ZA.at[:, theirs], vbs.at[0, my_rows, :])):
-            copy = pltpu.make_async_remote_copy(
-                src_ref=src, dst_ref=back[n],
-                send_sem=out_send.at[n, o], recv_sem=out_recv.at[n, o],
-                device_id=peers[o - 1], device_id_type=MESH,
-            )
-            copy.start()
-            rest.append(copy)
+        send_back(2, o, vbs.at[0, my_rows, :])
     for copy in finals:
         copy.wait()
     for copy in rest:
@@ -536,18 +586,20 @@
     def halo(length, packs):
         return [pltpu.VMEM((2, length, LANES), F32)] * 2 + [pltpu.VMEM((2, packs * ROWS, LANES), F32)] * 2
 
-    na, nb = ngx * 2, ngy * (ngz // 2)
+    na, nb = ngx * 2, (ngy // 2) * ngz
     scratch = (
-        [field, pltpu.VMEM((3, NZ, ROWS, LANES), F32), field]
+        [pltpu.VMEM((2, depth, rows, lanes), F32), pltpu.VMEM((rows, lanes), jnp.int32)]
+        + [pltpu.VMEM((ROWS, LANES), F32)] * 3
+        + [field, pltpu.VMEM((3, NZ, ROWS, LANES), F32), field]
         + [pltpu.VMEM((2, rows, lanes), F32), pltpu.VMEM((ngz, 2, ROWS, LANES), F32)]
         + [pltpu.VMEM((NZ + 1, ROWS, LANES), F32)]
         + [field] * 6
         + [state] * 6
         + halo(NZ + 8, 1) + halo(4 * NZ, 1) + halo(6 * NZ, 2) + halo(2 * NZ, 1)
-        + [pltpu.VMEM((2, ROWS, LANES), F32)]
-        + [pltpu.VMEM((na - 1, ROWS, LANES), F32), pltpu.VMEM((nb - 1, ROWS, LANES), F32)]
-        + [dma((4,)), dma((4, ngz)), dma((4, ngz)), dma((4, 4)), dma((4, 4))]
-        + [dma((2, max(na, nb))), dma((na,)), dma((nb,)), dma((3, ngz)), dma((3, ngz))]
+        + [pltpu.VMEM((2, ROWS, LANES), F32), pltpu.VMEM((2, 2, 1, LANES), F32)]
+        + [pltpu.VMEM((2, na - 1, 1, LANES), F32), pltpu.VMEM((2, nb - 1, 1, LANES), F32)]
+        + [dma((5,)), dma((4,)), dma((4, ngz)), dma((4, ngz)), dma((4, 4)), dma((4, 4))]
+        + [dma((2, 2, max(na, nb))), dma((2, na)), dma((2, nb)), dma((3, ngz)), dma((3, ngz))]
     )
     vmem = pl.BlockSpec(memory_space=pltpu.VMEM)
     hbm = pl.BlockSpec(memory_space=pl.ANY)
@@ -559,11 +611,11 @@
             jax.ShapeDtypeStruct((2, depth, rows, lanes), F32),
             jax.ShapeDtypeStruct((rows, lanes), F32),
         ),
-        in_specs=[vmem, hbm, hbm, hbm, vmem, vmem, vmem, smem, vmem],
+        in_specs=[hbm] * 7 + [smem, hbm],
         out_specs=(hbm, hbm, vmem),
         scratch_shapes=scratch,
         compiler_params=pltpu.CompilerParams(
-            collective_id=0, has_side_effects=True, vmem_limit_bytes=40 * 1024 * 1024
+            collective_id=0, has_side_effects=True, vmem_limit_bytes=62 * 1024 * 1024
         ),
     )(*args)
 

time: 88.2 us -> 72.3 us (0.82)
  the two profiles are of different devices: /device:TPU:1 before, /device:TPU:2 now
where the time goes in v2:
time: 72.3 us; the launch traced here: 72 us
  Pallas kernels  68 us (94%)
  local copies, waits for them, and re-layouts  3.36 us (5%)
    pallas_call x1, Pallas kernels, local(): pl.pallas_call(functools.partial(kernel, sizes), out_shape=(jax.ShapeDtyp...  68 us
    unnamed x7, local copies, waits for them, and re-layouts  3.36 us

profile of v2, /device:TPU:2, one launch (start us, length us, event | category | flops | bytes accessed | tf_op | source)
XLA Modules:
  0.0 72.0 jit_solution(8088101824037347328)
XLA Ops:
  0.6 68.0 %shard_map.112 = (f32[2,8,64,128]{3,2,1,0:T(8,128)}, f32[2,8,64,128]{3,2,1,0:T(8,128)}, f32[64,128]{1,0:T(8,128)}) custom-call(f32[2,8,64,128]{3,2,1,0:T(8,128)} %vel_in.1, f32[8,64,128]{2,1,0:T(8,128)} %visc.1, f32[3,8,64,128]{3,2,1,0:T(8,128)} %binv.1, f32[8,64,128]{2,1,0:T(8,128)} %coup.1, f32[64,128]{1,0:T(8,128)} %fric_in.1, f32[64,128]{1,0:T(8,128)} %fstep_in.1, ...), custom_call_target="tpu_custom_call" | custom-call | tf_op jit(solution)/shard_map/pallas_call | solution.py:607
  68.6 0.0 copy-start
  68.6 1.9 %copy.15 = f32[2,8,64,128]{3,2,1,0:T(8,128)} copy(f32[2,8,64,128]{3,2,1,0:T(8,128)} %get-tuple-element.6) | data formatting | bytes 1048576
  70.6 0.0 copy-done
  70.6 0.0 copy-start.1
  70.6 0.8 %copy.16 = f32[2,8,64,128]{3,2,1,0:T(8,128)} copy(f32[2,8,64,128]{3,2,1,0:T(8,128)S(1)} %copy-done) | data formatting | bytes 1048576
  71.4 0.0 copy-done.1
  71.4 0.6 copy.17
Async XLA Ops:
  68.6 2.0 %copy-start = (f32[2,8,64,128]{3,2,1,0:T(8,128)S(1)}, f32[2,8,64,128]{3,2,1,0:T(8,128)}, u32[]{:S(2)}) copy-start(f32[2,8,64,128]{3,2,1,0:T(8,128)} %get-tuple-element.7) | copy-start | bytes 1572868
  70.6 0.8 %copy-start.1 = (f32[64,128]{1,0:T(8,128)S(1)}, f32[64,128]{1,0:T(8,128)}, u32[]{:S(2)}) copy-start(f32[64,128]{1,0:T(8,128)} %get-tuple-element.8) | copy-start | bytes 98308

commit v3 on v2

--- a/solution.py
+++ b/solution.py
@@ -16,7 +16,7 @@
 NZ = 32
 ROWS = 16
 LANES = 128
-UNROLL = 8
+UNROLL = 32
 
 
 def blocked_loop(steps, body, carry):
@@ -43,39 +43,51 @@
     ngx, ngy, ngz = sizes
     gx, gy, gz = lax.axis_index("gx"), lax.axis_index("gy"), lax.axis_index("gz")
     depth = NZ // ngz
-    odd = gx % 2
+    odd = lax.rem(gx, 2)
+
+    def around(index, count):
+        return [index] + [lax.rem(index + o, count) for o in range(1, count)]
 
     def piece_of(q):
         return q + odd * (ngz - 1 - 2 * q)
 
-    piece = piece_of(gz)
+    gxs, gzs = around(gx, ngx), around(gz, ngz)
+    pieces = [piece_of(q) for q in gzs]
+    piece = pieces[0]
     total_pieces = ngx * ngz
     spot = gx * ngz + piece
 
     def holder(index):
-        block = index // ngz
-        part = index % ngz
-        return (block, gy, part + (block % 2) * (ngz - 1 - 2 * part))
-
-    x_low = holder((spot + total_pieces - 1) % total_pieces)
-    x_high = holder((spot + 1) % total_pieces)
-    y_low = (gx, (gy + ngy - 1) % ngy, gz)
-    y_high = (gx, (gy + 1) % ngy, gz)
-    peers = [(gx, gy, (gz + o) % ngz) for o in range(1, ngz)]
-    na, nb = ngx * 2, (ngy // 2) * ngz
-    core = gy % 2
-    ma, mb = gx * 2 + core, (gy // 2) * ngz + gz
-
-    def member_a(o):
-        m = (ma + o) % na
-        return (m // 2, (gy // 2) * 2 + m % 2, gz)
-
-    def member_b(o):
-        m = (mb + o) % nb
-        return (gx, (m // ngz) * 2 + core, m % ngz)
-
-    group_a = [member_a(o) for o in range(1, na)]
-    group_b = [member_b(o) for o in range(1, nb)]
+        block = lax.div(index, ngz)
+        part = index - block * ngz
+        return (block, gy, part + lax.rem(block, 2) * (ngz - 1 - 2 * part))
+
+    x_low = holder(lax.rem(spot + (total_pieces - 1), total_pieces))
+    x_high = holder(lax.rem(spot + 1, total_pieces))
+    y_low = (gx, lax.rem(gy + (ngy - 1), ngy), gz)
+    y_high = (gx, lax.rem(gy + 1, ngy), gz)
+    peers = [(gx, gy, q) for q in gzs[1:]]
+    chips = ngy // 2
+    na, nb = ngx * 2, chips * ngz
+    chip = lax.div(gy, 2)
+    core = gy - 2 * chip
+    same_core = [2 * c + core for c in around(chip, chips)]
+    other_core = 2 * chip + 1 - core
+    ma, mb = gx * 2 + core, chip * ngz + gz
+    y_other = (gx, lax.rem(gy + ngy + 2 * core - 1, ngy), gz)
+
+    def ring(offset, count):
+        return min(offset, count - offset)
+
+    steps_a = sorted(
+        ((i, j) for i in range(ngx) for j in range(2) if i or j), key=lambda step: -ring(step[0], ngx)
+    )
+    steps_b = sorted(
+        ((i, j) for i in range(chips) for j in range(ngz) if i or j),
+        key=lambda step: -ring(step[0], chips) - ring(step[1], ngz),
+    )
+    group_a = [(gxs[i], other_core if j else gy, gz) for i, j in steps_a]
+    group_b = [(gx, same_core[i], gzs[j]) for i, j in steps_b]
 
     here = pl.multiple_of(piece * ROWS, ROWS)
     my_rows = pl.ds(here, ROWS)
@@ -94,7 +106,9 @@
         loads.append(copy)
 
     barrier = pltpu.get_barrier_semaphore()
-    partners = [x_low, x_high, y_low, y_high] + peers + group_a + group_b
+    far = [(-ring(i, ngx), device) for (i, _), device in zip(steps_a, group_a)]
+    far += [(-ring(i, chips) - ring(j, ngz), device) for (i, j), device in zip(steps_b, group_b)]
+    partners = [device for _, device in sorted(far, key=lambda item: item[0])] + [y_other]
     for partner in partners:
         pl.semaphore_signal(barrier, inc=1, device_id=partner, device_id_type=MESH)
 
@@ -130,7 +144,7 @@
         copy.start()
         locals_in.append(copy)
     incoming = [[], [], [], []]
-    per_peer = [moves(piece_of((gz + o) % ngz), o) for o in range(1, ngz)]
+    per_peer = [moves(pieces[o], o) for o in range(1, ngz)]
     for a in range(4):
         for o in range(1, ngz):
             src, dst = per_peer[o - 1][a]
@@ -157,6 +171,7 @@
         for c in range(2):
             field[c, 0] = jnp.zeros((ROWS, LANES), F32)
             field[c, NZ + 1] = jnp.zeros((ROWS, LANES), F32)
+    V[NZ] = jnp.zeros((ROWS, LANES), F32)
     for ps in (ps0, ps3):
         ps[...] = jnp.zeros(ps.shape, F32)
 
@@ -217,42 +232,6 @@
     ps0[1] = high
     halo0 = send_halo(0, xs0, xr0, ps0, pr0)
 
-    for copy in halo0:
-        copy.wait_recv()
-    left, right = pr0[0], pr0[1]
-    bed_e, bed_w, bed_n, bed_s = beside(kbed, xr0, NZ, left, right, NZ)
-    bed_e = jnp.where((row == ROWS - 1) & (spot == total_pieces - 1), NONE, bed_e)
-    bed_w = jnp.where((row == 0) & (spot == 0), NONE, bed_w)
-    bed_n = jnp.where((lane == LANES - 1) & (gy == ngy - 1), NONE, bed_n)
-    bed_s = jnp.where((lane == 0) & (gy == 0), NONE, bed_s)
-
-    def layer_weights(k, carry):
-        below_v, below_a = carry
-        level = jnp.full((ROWS, LANES), k, jnp.int32).astype(F32)
-        value = V[k]
-        act = jnp.where(level >= kbed, 1.0, 0.0)
-        bedflag = jnp.where(level == kbed, 1.0, 0.0)
-        east, west, north, south = beside(value, xr0, k, left, right, k)
-        half_act = 0.5 * act
-        down = (VERTICAL * (value + below_v)) * (half_act * below_a)
-        we = (value + east) * jnp.where(level >= bed_e, half_act, 0.0)
-        ww = (value + west) * jnp.where(level >= bed_w, half_act, 0.0)
-        wn = (value + north) * jnp.where(level >= bed_n, half_act, 0.0)
-        ws = (value + south) * jnp.where(level >= bed_s, half_act, 0.0)
-        WU[k] = down
-        WE[k] = we
-        WW[k] = ww
-        WN[k] = wn
-        WS[k] = ws
-        ew, ns = we + ww, wn + ws
-        rest = friction * bedflag + (1.0 - act)
-        D0[k] = down + STRETCH * ew + ns + rest
-        D1[k] = down + ew + STRETCH * ns + rest
-        return value, act
-
-    blocked_loop(NZ, layer_weights, (blank, blank))
-    WU[NZ] = blank
-
     for group, copy in zip(incoming[1:], locals_in[1:]):
         copy.wait()
         for remote in group:
@@ -293,9 +272,6 @@
         at = level == kbed
         first = jnp.where(at, push0, 0.0)
         second = jnp.where(at, push1, 0.0)
-        above = WU[k + 1]
-        D0[k] = D0[k] + above
-        D1[k] = D1[k] + above
         return rise(k, first, second, state, Z0)
 
     state = blocked_loop(NZ, first_rise, (blank, blank, blank))
@@ -335,6 +311,42 @@
     ps1[1] = carry[5]
     halo1 = send_halo(1, xs1, xr1, ps1, pr1)
     raa = seed_a0 * ZA[0, NZ] + seed_a1 * ZA[1, NZ]
+
+    for copy in halo0:
+        copy.wait_recv()
+    left, right = pr0[0], pr0[1]
+    bed_e, bed_w, bed_n, bed_s = beside(kbed, xr0, NZ, left, right, NZ)
+    bed_e = jnp.where((row == ROWS - 1) & (spot == total_pieces - 1), NONE, bed_e)
+    bed_w = jnp.where((row == 0) & (spot == 0), NONE, bed_w)
+    bed_n = jnp.where((lane == LANES - 1) & (gy == ngy - 1), NONE, bed_n)
+    bed_s = jnp.where((lane == 0) & (gy == 0), NONE, bed_s)
+
+    def layer_weights(k, down):
+        level = jnp.full((ROWS, LANES), k, jnp.int32).astype(F32)
+        value = V[k]
+        act = jnp.where(level >= kbed, 1.0, 0.0)
+        above = jnp.where((level + 1.0 >= kbed) & (level + 1.0 < NZ), 1.0, 0.0)
+        bedflag = jnp.where(level == kbed, 1.0, 0.0)
+        east, west, north, south = beside(value, xr0, k, left, right, k)
+        half_act = 0.5 * act
+        up = (VERTICAL * (value + V[k + 1])) * (half_act * above)
+        we = (value + east) * jnp.where(level >= bed_e, half_act, 0.0)
+        ww = (value + west) * jnp.where(level >= bed_w, half_act, 0.0)
+        wn = (value + north) * jnp.where(level >= bed_n, half_act, 0.0)
+        ws = (value + south) * jnp.where(level >= bed_s, half_act, 0.0)
+        WU[k + 1] = up
+        WE[k] = we
+        WW[k] = ww
+        WN[k] = wn
+        WS[k] = ws
+        ew, ns = we + ww, wn + ws
+        rest = (up + down) + friction * bedflag + (1.0 - act)
+        D0[k] = STRETCH * ew + ns + rest
+        D1[k] = ew + STRETCH * ns + rest
+        return up
+
+    WU[0] = blank
+    blocked_loop(NZ, layer_weights, blank)
 
     def operate(k, weights, field, xr, xj, left, right, lj):
         up, down, we, ww, wn, ws, d0, d1 = weights
@@ -446,7 +458,7 @@
 
     d0, daa = blocked_loop(NZ, early_energy, (blank, blank))
 
-    stages = ((group_a, ra, red_recv_a), (group_b, rb, red_recv_b))
+    stages = ((group_a, ra, red_recv_a, ma), (group_b, rb, red_recv_b, mb))
 
     def gather_sums(values, turn):
         for n, value in enumerate(values):
@@ -456,11 +468,12 @@
 
     def send_sum(turn, stage, value):
         rt[turn, stage] = value
-        group, received, sem = stages[stage]
+        group, received, sem, place = stages[stage]
+        received[turn, place] = value
         copies = []
         for o, device in enumerate(group):
             copy = pltpu.make_async_remote_copy(
-                src_ref=rt.at[turn, stage], dst_ref=received.at[turn, o],
+                src_ref=rt.at[turn, stage], dst_ref=received.at[turn, place],
                 send_sem=red_send.at[turn, stage, o], recv_sem=sem.at[turn, o],
                 device_id=device, device_id_type=MESH,
             )
@@ -472,7 +485,7 @@
         for copy in copies:
             copy.wait_recv()
         received = stages[stage][1]
-        return rt[turn, stage] + jnp.sum(received[turn], axis=0)
+        return jnp.sum(received[turn], axis=0)
 
     def spread(total, count):
         each = jnp.sum(jnp.where(lane == row, total, 0.0), axis=1, keepdims=True)
@@ -526,7 +539,7 @@
         copy.start()
         finals.append(copy)
         for o in range(1, ngz):
-            theirs = pl.ds(1 + ((gz + o) % ngz) * depth, depth)
+            theirs = pl.ds(1 + gzs[o] * depth, depth)
             send_back(n, o, field.at[:, theirs])
 
     def send_back(n, o, src):
@@ -576,6 +589,19 @@
         copy.wait_send()
 
 
+def deliver(inc_in, adj_in, hess_in, inc, adj, hess, first, second, third, sem):
+    held = ((inc_in, first, inc), (adj_in, second, adj), (hess_in, third, hess))
+    reads = [pltpu.make_async_copy(src, mid, sem.at[n]) for n, (src, mid, _) in enumerate(held)]
+    writes = [pltpu.make_async_copy(mid, dst, sem.at[n + 3]) for n, (_, mid, dst) in enumerate(held)]
+    for copy in reads:
+        copy.start()
+    for read, write in zip(reads, writes):
+        read.wait()
+        write.start()
+    for copy in writes:
+        copy.wait()
+
+
 def local(sizes, *args):
     ngx, ngy, ngz = sizes
     field = pltpu.VMEM((NZ, ROWS, LANES), F32)
@@ -590,27 +616,28 @@
     scratch = (
         [pltpu.VMEM((2, depth, rows, lanes), F32), pltpu.VMEM((rows, lanes), jnp.int32)]
         + [pltpu.VMEM((ROWS, LANES), F32)] * 3
-        + [field, pltpu.VMEM((3, NZ, ROWS, LANES), F32), field]
+        + [pltpu.VMEM((NZ + 1, ROWS, LANES), F32), pltpu.VMEM((3, NZ, ROWS, LANES), F32), field]
         + [pltpu.VMEM((2, rows, lanes), F32), pltpu.VMEM((ngz, 2, ROWS, LANES), F32)]
         + [pltpu.VMEM((NZ + 1, ROWS, LANES), F32)]
         + [field] * 6
         + [state] * 6
         + halo(NZ + 8, 1) + halo(4 * NZ, 1) + halo(6 * NZ, 2) + halo(2 * NZ, 1)
         + [pltpu.VMEM((2, ROWS, LANES), F32), pltpu.VMEM((2, 2, 1, LANES), F32)]
-        + [pltpu.VMEM((2, na - 1, 1, LANES), F32), pltpu.VMEM((2, nb - 1, 1, LANES), F32)]
+        + [pltpu.VMEM((2, na, 1, LANES), F32), pltpu.VMEM((2, nb, 1, LANES), F32)]
         + [dma((5,)), dma((4,)), dma((4, ngz)), dma((4, ngz)), dma((4, 4)), dma((4, 4))]
         + [dma((2, 2, max(na, nb))), dma((2, na)), dma((2, nb)), dma((3, ngz)), dma((3, ngz))]
     )
     vmem = pl.BlockSpec(memory_space=pltpu.VMEM)
     hbm = pl.BlockSpec(memory_space=pl.ANY)
     smem = pl.BlockSpec(memory_space=pltpu.SMEM)
-    return pl.pallas_call(
+    shapes = (
+        jax.ShapeDtypeStruct((2, depth, rows, lanes), F32),
+        jax.ShapeDtypeStruct((2, depth, rows, lanes), F32),
+        jax.ShapeDtypeStruct((rows, lanes), F32),
+    )
+    results = pl.pallas_call(
         functools.partial(kernel, sizes),
-        out_shape=(
-            jax.ShapeDtypeStruct((2, depth, rows, lanes), F32),
-            jax.ShapeDtypeStruct((2, depth, rows, lanes), F32),
-            jax.ShapeDtypeStruct((rows, lanes), F32),
-        ),
+        out_shape=shapes,
         in_specs=[hbm] * 7 + [smem, hbm],
         out_specs=(hbm, hbm, vmem),
         scratch_shapes=scratch,
@@ -618,6 +645,14 @@
             collective_id=0, has_side_effects=True, vmem_limit_bytes=62 * 1024 * 1024
         ),
     )(*args)
+    return pl.pallas_call(
+        deliver,
+        out_shape=shapes,
+        in_specs=[hbm] * 3,
+        out_specs=(hbm, hbm, hbm),
+        scratch_shapes=[pltpu.VMEM(shape.shape, F32) for shape in shapes] + [dma((6,))],
+        compiler_params=pltpu.CompilerParams(vmem_limit_bytes=62 * 1024 * 1024),
+    )(*results)
 
 
 def solution(mesh):

time: 72.3 us -> 68.9 us (0.953)
  local copies, waits for them, and re-layouts: 3.36 us -> 0 us
    unnamed x7 -> x0, local copies, waits for them, and re-layouts: 3.36 us -> none
    pallas_call x1 -> x2, Pallas kernels: 68 us -> 68 us  [the longest x1 65.9 us: local(): pl.pallas_call(functools.partial(kernel, sizes), out_shape=shapes, in_spe...]
where the time goes in v3:
time: 68.9 us; the launch traced here: 68.6 us
  Pallas kernels  68 us (99%)
    pallas_call x1, Pallas kernels, local(): pl.pallas_call(functools.partial(kernel, sizes), out_shape=shapes, in_spe...  65.9 us
    pallas_call x1, Pallas kernels, local(): pl.pallas_call(deliver, out_shape=shapes, in_specs=[hbm] * 3, out_specs=(...  2.06 us

profile of v3, /device:TPU:2, one launch (start us, length us, event | category | flops | bytes accessed | tf_op | source)
XLA Modules:
  0.0 68.6 jit_solution(4791108532269178996)
XLA Ops:
  0.6 65.9 %shard_map.112 = (f32[2,8,64,128]{3,2,1,0:T(8,128)}, f32[2,8,64,128]{3,2,1,0:T(8,128)}, f32[64,128]{1,0:T(8,128)}) custom-call(f32[2,8,64,128]{3,2,1,0:T(8,128)} %vel_in.1, f32[8,64,128]{2,1,0:T(8,128)} %visc.1, f32[3,8,64,128]{3,2,1,0:T(8,128)} %binv.1, f32[8,64,128]{2,1,0:T(8,128)} %coup.1, f32[64,128]{1,0:T(8,128)} %fric_in.1, f32[64,128]{1,0:T(8,128)} %fstep_in.1, ...), custom_call_target="tpu_custom_call" | custom-call | tf_op jit(solution)/shard_map/pallas_call | solution.py:638
  66.6 2.1 %shard_map.113 = (f32[2,8,64,128]{3,2,1,0:T(8,128)}, f32[2,8,64,128]{3,2,1,0:T(8,128)}, f32[64,128]{1,0:T(8,128)}) custom-call(f32[2,8,64,128]{3,2,1,0:T(8,128)} %get-tuple-element.6.inc_in, f32[2,8,64,128]{3,2,1,0:T(8,128)} %get-tuple-element.7.adj_in, f32[64,128]{1,0:T(8,128)} %get-tuple-element.8.hess_in), custom_call_target="tpu_custom_call" | custom-call | tf_op jit(solution)/shard_map/pallas_call | solution.py:648

commit v4 on v3

--- a/solution.py
+++ b/solution.py
@@ -33,11 +33,11 @@
     vel_in, visc, binv, coup, fric_in, fstep_in, misfit_in, ice, bed_in,
     inc, adj, hess,
     vel, bed, fric, fstep, misfit,
-    V, B, L, vbs, vbp, WU, WE, WW, WN, WS, D0, D1,
+    FX, V, B, L, vbs, vbp, WU, WE, WW, WN, WS, D0, D1,
     Z0, ZA, S0, SA, ZB, SB,
     xs0, xr0, ps0, pr0, xs1, xr1, ps1, pr1, xs2, xr2, ps2, pr2, xs3, xr3, ps3, pr3,
     stack, rt, ra, rb,
-    load_sem, loc_sem, in_send, in_recv, halo_send, halo_recv, red_send, red_recv_a, red_recv_b,
+    gathered, load_sem, loc_sem, in_send, in_recv, halo_send, halo_recv, red_send, red_recv_a, red_recv_b,
     out_send, out_recv,
 ):
     ngx, ngy, ngz = sizes
@@ -145,7 +145,7 @@
         locals_in.append(copy)
     incoming = [[], [], [], []]
     per_peer = [moves(pieces[o], o) for o in range(1, ngz)]
-    for a in range(4):
+    for a in (3, 1, 2, 0):
         for o in range(1, ngz):
             src, dst = per_peer[o - 1][a]
             copy = pltpu.make_async_remote_copy(
@@ -204,34 +204,7 @@
             copies.append(copy)
         return copies
 
-    def beside(value, xr, xj, left, right, lj):
-        east = jnp.where(row == ROWS - 1, xr[1, pl.ds(xj, 1), :], pltpu.roll(value, ROWS - 1, 0))
-        west = jnp.where(row == 0, xr[0, pl.ds(xj, 1), :], pltpu.roll(value, 1, 0))
-        north = jnp.where(
-            lane == LANES - 1, pltpu.roll(right, LANES - 1 - lj, 1), pltpu.roll(value, LANES - 1, 1)
-        )
-        south = jnp.where(
-            lane == 0, pltpu.roll(left, (LANES - lj) % LANES, 1), pltpu.roll(value, 1, 1)
-        )
-        return east, west, north, south
-
-    locals_in[0].wait()
-    for copy in incoming[0]:
-        copy.wait_recv()
-
-    def pack_viscosity(k, packed):
-        value = V[k]
-        pack_rows(xs0, value, k)
-        return pack_lane(packed, value, k)
-
     blank = jnp.zeros((ROWS, LANES), F32)
-    packed = blocked_loop(NZ, pack_viscosity, (blank, blank))
-    pack_rows(xs0, kbed, NZ)
-    low, high = pack_lane(packed, kbed, NZ)
-    ps0[0] = low
-    ps0[1] = high
-    halo0 = send_halo(0, xs0, xr0, ps0, pr0)
-
     for group, copy in zip(incoming[1:], locals_in[1:]):
         copy.wait()
         for remote in group:
@@ -312,14 +285,34 @@
     halo1 = send_halo(1, xs1, xr1, ps1, pr1)
     raa = seed_a0 * ZA[0, NZ] + seed_a1 * ZA[1, NZ]
 
-    for copy in halo0:
+    locals_in[0].wait()
+    for copy in incoming[0]:
         copy.wait_recv()
-    left, right = pr0[0], pr0[1]
-    bed_e, bed_w, bed_n, bed_s = beside(kbed, xr0, NZ, left, right, NZ)
-    bed_e = jnp.where((row == ROWS - 1) & (spot == total_pieces - 1), NONE, bed_e)
-    bed_w = jnp.where((row == 0) & (spot == 0), NONE, bed_w)
-    bed_n = jnp.where((lane == LANES - 1) & (gy == ngy - 1), NONE, bed_n)
-    bed_s = jnp.where((lane == 0) & (gy == 0), NONE, bed_s)
+
+    def pack_viscosity(k, packed):
+        value = V[k]
+        pack_rows(xs0, value, k)
+        return pack_lane(packed, value, k)
+
+    packed = blocked_loop(NZ, pack_viscosity, (blank, blank))
+    pack_rows(xs0, kbed, NZ)
+    low, high = pack_lane(packed, kbed, NZ)
+    ps0[0] = low
+    ps0[1] = high
+    halo0 = send_halo(0, xs0, xr0, ps0, pr0)
+
+    def beside(value):
+        east = pltpu.roll(value, ROWS - 1, 0)
+        west = pltpu.roll(value, 1, 0)
+        north = pltpu.roll(value, LANES - 1, 1)
+        south = pltpu.roll(value, 1, 1)
+        return east, west, north, south
+
+    bed_e, bed_w, bed_n, bed_s = beside(kbed)
+    bed_e = jnp.where(row == ROWS - 1, NONE, bed_e)
+    bed_w = jnp.where(row == 0, NONE, bed_w)
+    bed_n = jnp.where(lane == LANES - 1, NONE, bed_n)
+    bed_s = jnp.where(lane == 0, NONE, bed_s)
 
     def layer_weights(k, down):
         level = jnp.full((ROWS, LANES), k, jnp.int32).astype(F32)
@@ -327,7 +320,7 @@
         act = jnp.where(level >= kbed, 1.0, 0.0)
         above = jnp.where((level + 1.0 >= kbed) & (level + 1.0 < NZ), 1.0, 0.0)
         bedflag = jnp.where(level == kbed, 1.0, 0.0)
-        east, west, north, south = beside(value, xr0, k, left, right, k)
+        east, west, north, south = beside(value)
         half_act = 0.5 * act
         up = (VERTICAL * (value + V[k + 1])) * (half_act * above)
         we = (value + east) * jnp.where(level >= bed_e, half_act, 0.0)
@@ -348,14 +341,12 @@
     WU[0] = blank
     blocked_loop(NZ, layer_weights, blank)
 
-    def operate(k, weights, field, xr, xj, left, right, lj):
+    def operate(k, weights, field):
         up, down, we, ww, wn, ws, d0, d1 = weights
         result = []
         for c in range(2):
             value = field[c, k + 1]
-            east, west, north, south = beside(
-                value, xr, xj + c * NZ + k, left, right, lj + c * NZ + k
-            )
+            east, west, north, south = beside(value)
             vertical = up * field[c, k + 2] + down * field[c, k]
             ew = we * east + ww * west
             ns = wn * north + ws * south
@@ -365,21 +356,91 @@
                 result.append(d1 * value - vertical - ew - STRETCH * ns)
         return result
 
+    def keep(k, weights, field, out):
+        image = operate(k, weights, field)
+        out[0, k + 1] = image[0]
+        out[1, k + 1] = image[1]
+
+    def complete(k, inner, xr, low, high, n, lanes_from):
+        return [
+            inner[c, k + 1] + shared(xr, NZ * (n + c) + k, low, high, lanes_from + NZ * c + k)
+            for c in range(2)
+        ]
+
     def weights_of(k):
         return WU[k + 1], WU[k], WE[k], WW[k], WN[k], WS[k], D0[k], D1[k]
 
     def against(field, k, image, total):
         return total + (field[0, k + 1] * image[0] + field[1, k + 1] * image[1])
 
+    def inner_first(k, carry):
+        weights = weights_of(k)
+        keep(k, weights, Z0, S0)
+        keep(k, weights, ZA, SA)
+        return carry
+
+    blocked_loop(NZ, inner_first, 0)
+    for copy in halo0:
+        copy.wait_recv()
+    rows_level = lax.broadcasted_iota(jnp.int32, (NZ, LANES), 0).astype(F32)
+    lanes_level = lane.astype(F32)
+    x_edges = (spot == 0, spot == total_pieces - 1)
+    y_edges = (gy == 0, gy == ngy - 1)
+    FY = []
+    for side in range(2):
+        own_bed = xs0[side, NZ : NZ + 1, :]
+        their_bed = jnp.where(x_edges[side], NONE, xr0[side, NZ : NZ + 1, :])
+        both = (rows_level >= own_bed) & (rows_level >= their_bed)
+        face = jnp.where(both, 0.5 * (xs0[side, :NZ, :] + xr0[side, :NZ, :]), 0.0)
+        FX[side, :NZ, :] = STRETCH * face
+        FX[side, NZ:, :] = face
+        own, theirs = ps0[side], pr0[side]
+        own_bed = jnp.sum(jnp.where(lane == NZ, own, 0.0), axis=1, keepdims=True)
+        their_bed = jnp.sum(jnp.where(lane == NZ, theirs, 0.0), axis=1, keepdims=True)
+        their_bed = jnp.where(y_edges[side], NONE, their_bed)
+        both = (lanes_level >= own_bed) & (lanes_level >= their_bed) & (lane < NZ)
+        face = jnp.where(both, 0.5 * (own + theirs), 0.0)
+        face = face + STRETCH * pltpu.roll(face, NZ, 1)
+        FY.append(face + pltpu.roll(face, 2 * NZ, 1))
+
+    def exchange(xs, xr, ps, pr, fields, packs):
+        for side in range(2):
+            for n in range(fields):
+                part = pl.ds(2 * NZ * n, 2 * NZ)
+                xr[side, part, :] = FX[side] * (xs[side, part, :] - xr[side, part, :])
+            for n in range(packs):
+                part = pl.ds(ROWS * n, ROWS)
+                pr[side, part, :] = FY[side] * (ps[side, part, :] - pr[side, part, :])
+
+    def shared(xr, xj, low, high, lj):
+        result = jnp.where(row == 0, xr[0, pl.ds(xj, 1), :], 0.0)
+        result = jnp.where(row == ROWS - 1, xr[1, pl.ds(xj, 1), :], result)
+        result = result + jnp.where(lane == 0, pltpu.roll(low, lax.rem(LANES - lj, LANES), 1), 0.0)
+        return result + jnp.where(lane == LANES - 1, pltpu.roll(high, LANES - 1 - lj, 1), 0.0)
+
+    def shared_energy(xs, ps, first, pack, start, xr, pr, xr_first, pr_pack, pr_start):
+        total = blank
+        for side in range(2):
+            for n in range(2 * NZ // ROWS):
+                mine = xs[side, pl.ds(2 * NZ * first + ROWS * n, ROWS), :]
+                total = total + mine * xr[side, pl.ds(2 * NZ * xr_first + ROWS * n, ROWS), :]
+            mine = ps[side, pl.ds(ROWS * pack, ROWS), :]
+            theirs = pr[side, pl.ds(ROWS * pr_pack, ROWS), :]
+            if start != pr_start:
+                mine = pltpu.roll(mine, (pr_start - start) % LANES, 1)
+            inside = (lane >= pr_start) & (lane < pr_start + 2 * NZ)
+            total = total + jnp.where(inside, mine * theirs, 0.0)
+        return total
+
     for copy in halo1:
         copy.wait_recv()
-    left1, right1 = pr1[0], pr1[1]
+    exchange(xs1, xr1, ps1, pr1, 2, 1)
+    low1, high1 = pr1[0], pr1[1]
 
     def middle_rise(k, carry):
         pq0, paa, main, extra = carry
-        weights = weights_of(k)
-        w = operate(k, weights, Z0, xr1, 0, left1, right1, 0)
-        wa = operate(k, weights, ZA, xr1, 2 * NZ, left1, right1, 2 * NZ)
+        w = complete(k, S0, xr1, low1, high1, 0, 0)
+        wa = complete(k, SA, xr1, low1, high1, 2, 2 * NZ)
         pq0 = against(Z0, k, w, pq0)
         paa = against(ZA, k, wa, paa)
         main = rise(k, w[0], w[1], main, S0)
@@ -417,14 +478,23 @@
     rab = seed_a0 * ZB[0, NZ] + seed_a1 * ZB[1, NZ]
     rbb = seed_b0 * ZB[0, NZ] + seed_b1 * ZB[1, NZ]
 
+    def inner_second(k, carry):
+        d0, daa = carry
+        weights = weights_of(k)
+        keep(k, weights, ZB, SB)
+        d0 = against(S0, k, operate(k, weights, S0), d0)
+        daa = against(SA, k, operate(k, weights, SA), daa)
+        return d0, daa
+
+    d0, daa = blocked_loop(NZ, inner_second, (blank, blank))
     for copy in halo2:
         copy.wait_recv()
-    left2, right2 = pr2[0, :ROWS, :], pr2[1, :ROWS, :]
-    left3, right3 = pr2[0, ROWS:, :], pr2[1, ROWS:, :]
+    exchange(xs2, xr2, ps2, pr2, 3, 2)
+    low2, high2 = pr2[0, :ROWS, :], pr2[1, :ROWS, :]
 
     def last_rise(k, carry):
         pab, pbb, gab, main = carry
-        w = operate(k, weights_of(k), ZB, xr2, 0, left2, right2, 0)
+        w = complete(k, SB, xr2, low2, high2, 0, 0)
         pab = against(ZA, k, w, pab)
         pbb = against(ZB, k, w, pbb)
         gab = against(SA, k, w, gab)
@@ -449,14 +519,35 @@
     ps3[1] = carry[3]
     halo3 = send_halo(3, xs3, xr3, ps3, pr3)
 
-    def early_energy(k, carry):
-        d0, daa = carry
-        weights = weights_of(k)
-        w = operate(k, weights, S0, xr2, 2 * NZ, left2, right2, 2 * NZ)
-        wa = operate(k, weights, SA, xr2, 4 * NZ, left3, right3, 0)
-        return against(S0, k, w, d0), against(SA, k, wa, daa)
-
-    d0, daa = blocked_loop(NZ, early_energy, (blank, blank))
+    finals = []
+    rest = []
+    places = [
+        gathered.at[0, :, :, my_rows, :],
+        gathered.at[1, :, :, my_rows, :],
+        adj.at[:, :, my_rows, :],
+        hess.at[my_rows, :],
+    ]
+
+    def give_back(n, field):
+        for o in range(1, ngz):
+            send_back(n, o, field.at[:, pl.ds(1 + gzs[o] * depth, depth)])
+        copy = pltpu.make_async_copy(field.at[:, pl.ds(1 + base, depth)], places[n], loc_sem.at[n])
+        copy.start()
+        finals.append(copy)
+
+    def send_back(n, o, src):
+        copy = pltpu.make_async_remote_copy(
+            src_ref=src, dst_ref=places[n],
+            send_sem=out_send.at[n, o], recv_sem=out_recv.at[n, o],
+            device_id=peers[o - 1], device_id_type=MESH,
+        )
+        copy.start()
+        rest.append(copy)
+
+    give_back(0, Z0)
+    give_back(1, S0)
+    d0 = d0 + shared_energy(xs2, ps2, 1, 0, 2 * NZ, xr2, pr2, 1, 0, 2 * NZ)
+    daa = daa + shared_energy(xs2, ps2, 2, 1, 0, xr2, pr2, 2, 1, 0)
 
     stages = ((group_a, ra, red_recv_a, ma), (group_b, rb, red_recv_b, mb))
 
@@ -495,17 +586,17 @@
     stack[...] = jnp.zeros(stack.shape, F32)
     first_a = send_sum(0, 0, gather_sums([rz0, pq0, g0, d0], 0))
 
+    def inner_third(k, carry):
+        dab, dbb = carry
+        image = operate(k, weights_of(k), SB)
+        return against(SA, k, image, dab), against(SB, k, image, dbb)
+
+    dab, dbb = blocked_loop(NZ, inner_third, (blank, blank))
     for copy in halo3:
         copy.wait_recv()
-    left4, right4 = pr3[0], pr3[1]
-
-    def late_energy(k, carry):
-        dab, dbb = carry
-        w = operate(k, weights_of(k), SB, xr3, 0, left4, right4, 0)
-        return against(SA, k, w, dab), against(SB, k, w, dbb)
-
-    dab, dbb = blocked_loop(NZ, late_energy, (blank, blank))
-
+    exchange(xs3, xr3, ps3, pr3, 1, 1)
+    dab = dab + shared_energy(xs2, ps2, 2, 1, 0, xr3, pr3, 0, 0, 0)
+    dbb = dbb + shared_energy(xs3, ps3, 0, 0, 0, xr3, pr3, 0, 0, 0)
     second_a = send_sum(
         1, 0, gather_sums([raa, rab, rbb, paa, pab, pbb, gaa, gab, gbb, daa, dab, dbb], 1)
     )
@@ -524,34 +615,20 @@
 
     c0, c1 = combination(rz0, pq0, g0, d0)
 
+    for copy in finals:
+        copy.wait()
+    for copy in rest:
+        copy.wait_recv()
+
     def increments(k, carry):
         for c in range(2):
-            Z0[c, k + 1] = c0 * Z0[c, k + 1] + c1 * S0[c, k + 1]
+            gathered[0, c, k] = c0 * gathered[0, c, k] + c1 * gathered[1, c, k]
         return carry
 
-    blocked_loop(NZ, increments, 0)
-    finals = []
-    rest = []
-    back = (inc.at[:, :, my_rows, :], adj.at[:, :, my_rows, :], hess.at[my_rows, :])
-
-    def give_back(n, field):
-        copy = pltpu.make_async_copy(field.at[:, pl.ds(1 + base, depth)], back[n], loc_sem.at[n])
-        copy.start()
-        finals.append(copy)
-        for o in range(1, ngz):
-            theirs = pl.ds(1 + gzs[o] * depth, depth)
-            send_back(n, o, field.at[:, theirs])
-
-    def send_back(n, o, src):
-        copy = pltpu.make_async_remote_copy(
-            src_ref=src, dst_ref=back[n],
-            send_sem=out_send.at[n, o], recv_sem=out_recv.at[n, o],
-            device_id=peers[o - 1], device_id_type=MESH,
-        )
-        copy.start()
-        rest.append(copy)
-
-    give_back(0, Z0)
+    lax.fori_loop(0, depth, increments, 0)
+    landed = len(rest)
+    finals = [pltpu.make_async_copy(gathered.at[0], inc, loc_sem.at[3])]
+    finals[0].start()
 
     raa, rab, rbb, paa, pab, pbb, gaa, gab, gbb, daa, dab, dbb = spread(finish_sum(1, 1, second_b), 12)
 
@@ -572,16 +649,18 @@
         return tuple(out)
 
     basal = blocked_loop(NZ, adjoints, (blank, blank))
-    give_back(1, ZA)
+    give_back(2, ZA)
     action = friction * (speed0 * basal[0] + speed1 * basal[1])
     hess[my_rows, :] = action
     vbs[0, my_rows, :] = action
     for o in range(1, ngz):
-        send_back(2, o, vbs.at[0, my_rows, :])
+        send_back(3, o, vbs.at[0, my_rows, :])
     for copy in finals:
         copy.wait()
+    for copy in rest[landed:]:
+        copy.wait_recv()
     for copy in rest:
-        copy.wait()
+        copy.wait_send()
     for group in incoming:
         for copy in group:
             copy.wait_send()
@@ -616,6 +695,7 @@
     scratch = (
         [pltpu.VMEM((2, depth, rows, lanes), F32), pltpu.VMEM((rows, lanes), jnp.int32)]
         + [pltpu.VMEM((ROWS, LANES), F32)] * 3
+        + [pltpu.VMEM((2, 2 * NZ, LANES), F32)]
         + [pltpu.VMEM((NZ + 1, ROWS, LANES), F32), pltpu.VMEM((3, NZ, ROWS, LANES), F32), field]
         + [pltpu.VMEM((2, rows, lanes), F32), pltpu.VMEM((ngz, 2, ROWS, LANES), F32)]
         + [pltpu.VMEM((NZ + 1, ROWS, LANES), F32)]
@@ -624,8 +704,9 @@
         + halo(NZ + 8, 1) + halo(4 * NZ, 1) + halo(6 * NZ, 2) + halo(2 * NZ, 1)
         + [pltpu.VMEM((2, ROWS, LANES), F32), pltpu.VMEM((2, 2, 1, LANES), F32)]
         + [pltpu.VMEM((2, na, 1, LANES), F32), pltpu.VMEM((2, nb, 1, LANES), F32)]
+        + [pltpu.VMEM((2, 2, depth, rows, lanes), F32)]
         + [dma((5,)), dma((4,)), dma((4, ngz)), dma((4, ngz)), dma((4, 4)), dma((4, 4))]
-        + [dma((2, 2, max(na, nb))), dma((2, na)), dma((2, nb)), dma((3, ngz)), dma((3, ngz))]
+        + [dma((2, 2, max(na, nb))), dma((2, na)), dma((2, nb)), dma((4, ngz)), dma((4, ngz))]
     )
     vmem = pl.BlockSpec(memory_space=pltpu.VMEM)
     hbm = pl.BlockSpec(memory_space=pl.ANY)

time: 68.9 us -> 65.5 us (0.951)
  Pallas kernels: 68 us -> 64.7 us
    pallas_call x1, Pallas kernels: 65.9 us -> 62.6 us  [local(): pl.pallas_call(functools.partial(kernel, sizes), out_shape=shapes, in_spe...]
where the time goes in v4:
time: 65.5 us; the launch traced here: 65.3 us
  Pallas kernels  64.7 us (99%)
    pallas_call x1, Pallas kernels, local(): pl.pallas_call(functools.partial(kernel, sizes), out_shape=shapes, in_spe...  62.6 us
    pallas_call x1, Pallas kernels, local(): pl.pallas_call(deliver, out_shape=shapes, in_specs=[hbm] * 3, out_specs=(...  2.06 us

profile of v4, /device:TPU:2, one launch (start us, length us, event | category | flops | bytes accessed | tf_op | source)
XLA Modules:
  0.0 65.3 jit_solution(13896327553937731323)
XLA Ops:
  0.6 62.6 %shard_map.112 = (f32[2,8,64,128]{3,2,1,0:T(8,128)}, f32[2,8,64,128]{3,2,1,0:T(8,128)}, f32[64,128]{1,0:T(8,128)}) custom-call(f32[2,8,64,128]{3,2,1,0:T(8,128)} %vel_in.1, f32[8,64,128]{2,1,0:T(8,128)} %visc.1, f32[3,8,64,128]{3,2,1,0:T(8,128)} %binv.1, f32[8,64,128]{2,1,0:T(8,128)} %coup.1, f32[64,128]{1,0:T(8,128)} %fric_in.1, f32[64,128]{1,0:T(8,128)} %fstep_in.1, ...), custom_call_target="tpu_custom_call" | custom-call | tf_op jit(solution)/shard_map/pallas_call | solution.py:719
  63.3 2.1 %shard_map.113 = (f32[2,8,64,128]{3,2,1,0:T(8,128)}, f32[2,8,64,128]{3,2,1,0:T(8,128)}, f32[64,128]{1,0:T(8,128)}) custom-call(f32[2,8,64,128]{3,2,1,0:T(8,128)} %get-tuple-element.6.inc_in, f32[2,8,64,128]{3,2,1,0:T(8,128)} %get-tuple-element.7.adj_in, f32[64,128]{1,0:T(8,128)} %get-tuple-element.8.hess_in), custom_call_target="tpu_custom_call" | custom-call | tf_op jit(solution)/shard_map/pallas_call | solution.py:729

commit v5 on v4

--- a/solution.py
+++ b/solution.py
@@ -146,7 +146,7 @@
     incoming = [[], [], [], []]
     per_peer = [moves(pieces[o], o) for o in range(1, ngz)]
     for a in (3, 1, 2, 0):
-        for o in range(1, ngz):
+        for o in (2, 1, 3):
             src, dst = per_peer[o - 1][a]
             copy = pltpu.make_async_remote_copy(
                 src_ref=src, dst_ref=dst,
@@ -551,40 +551,37 @@
 
     stages = ((group_a, ra, red_recv_a, ma), (group_b, rb, red_recv_b, mb))
 
-    def gather_sums(values, turn):
+    def gather_sums(values):
         for n, value in enumerate(values):
-            stack[turn, n : n + 1, :] = jnp.sum(value, axis=0, keepdims=True)
-        each = jnp.sum(stack[turn], axis=1, keepdims=True)
+            stack[n : n + 1, :] = jnp.sum(value, axis=0, keepdims=True)
+        each = jnp.sum(stack[...], axis=1, keepdims=True)
         return jnp.sum(jnp.where(lane == row, each, 0.0), axis=0, keepdims=True)
 
-    def send_sum(turn, stage, value):
-        rt[turn, stage] = value
+    def send_sum(stage, value):
+        rt[stage] = value
         group, received, sem, place = stages[stage]
-        received[turn, place] = value
+        received[place] = value
         copies = []
         for o, device in enumerate(group):
             copy = pltpu.make_async_remote_copy(
-                src_ref=rt.at[turn, stage], dst_ref=received.at[turn, place],
-                send_sem=red_send.at[turn, stage, o], recv_sem=sem.at[turn, o],
+                src_ref=rt.at[stage], dst_ref=received.at[place],
+                send_sem=red_send.at[stage, o], recv_sem=sem.at[o],
                 device_id=device, device_id_type=MESH,
             )
             copy.start()
             copies.append(copy)
         return copies
 
-    def finish_sum(turn, stage, copies):
+    def finish_sum(stage, copies):
         for copy in copies:
             copy.wait_recv()
-        received = stages[stage][1]
-        return jnp.sum(received[turn], axis=0)
+        return jnp.sum(stages[stage][1][...], axis=0)
 
     def spread(total, count):
         each = jnp.sum(jnp.where(lane == row, total, 0.0), axis=1, keepdims=True)
         each = jnp.broadcast_to(each, (ROWS, LANES))
         return [each[n : n + 1, :] for n in range(count)]
 
-    stack[...] = jnp.zeros(stack.shape, F32)
-    first_a = send_sum(0, 0, gather_sums([rz0, pq0, g0, d0], 0))
 
     def inner_third(k, carry):
         dab, dbb = carry
@@ -597,13 +594,11 @@
     exchange(xs3, xr3, ps3, pr3, 1, 1)
     dab = dab + shared_energy(xs2, ps2, 2, 1, 0, xr3, pr3, 0, 0, 0)
     dbb = dbb + shared_energy(xs3, ps3, 0, 0, 0, xr3, pr3, 0, 0, 0)
-    second_a = send_sum(
-        1, 0, gather_sums([raa, rab, rbb, paa, pab, pbb, gaa, gab, gbb, daa, dab, dbb], 1)
-    )
-    first_b = send_sum(0, 1, finish_sum(0, 0, first_a))
-    second_b = send_sum(1, 1, finish_sum(1, 0, second_a))
-    reductions = first_a + second_a + first_b + second_b
-    rz0, pq0, g0, d0 = spread(finish_sum(0, 1, first_b), 4)
+    sums = [rz0, pq0, g0, d0, raa, rab, rbb, paa, pab, pbb, gaa, gab, gbb, daa, dab, dbb]
+    first = send_sum(0, gather_sums(sums))
+    second = send_sum(1, finish_sum(0, first))
+    reductions = first + second
+    (rz0, pq0, g0, d0, raa, rab, rbb, paa, pab, pbb, gaa, gab, gbb, daa, dab, dbb) = spread(finish_sum(1, second), 16)
 
     def combination(rz, pq, g, d):
         step = rz / pq
@@ -614,23 +609,6 @@
         return step + second * grow, -(second * step)
 
     c0, c1 = combination(rz0, pq0, g0, d0)
-
-    for copy in finals:
-        copy.wait()
-    for copy in rest:
-        copy.wait_recv()
-
-    def increments(k, carry):
-        for c in range(2):
-            gathered[0, c, k] = c0 * gathered[0, c, k] + c1 * gathered[1, c, k]
-        return carry
-
-    lax.fori_loop(0, depth, increments, 0)
-    landed = len(rest)
-    finals = [pltpu.make_async_copy(gathered.at[0], inc, loc_sem.at[3])]
-    finals[0].start()
-
-    raa, rab, rbb, paa, pab, pbb, gaa, gab, gbb, daa, dab, dbb = spread(finish_sum(1, 1, second_b), 12)
 
     def form(aa, ab, bb):
         return c0 * c0 * aa + 2.0 * (c0 * c1) * ab + c1 * c1 * bb
@@ -648,6 +626,7 @@
             out.append(jnp.where(at, value, carry[c]))
         return tuple(out)
 
+    landed = len(rest)
     basal = blocked_loop(NZ, adjoints, (blank, blank))
     give_back(2, ZA)
     action = friction * (speed0 * basal[0] + speed1 * basal[1])
@@ -655,7 +634,21 @@
     vbs[0, my_rows, :] = action
     for o in range(1, ngz):
         send_back(3, o, vbs.at[0, my_rows, :])
-    for copy in finals:
+    for copy in finals[:2]:
+        copy.wait()
+    for copy in rest[:landed]:
+        copy.wait_recv()
+
+    def increments(k, carry):
+        for c in range(2):
+            gathered[0, c, k] = c0 * gathered[0, c, k] + c1 * gathered[1, c, k]
+        return carry
+
+    lax.fori_loop(0, depth, increments, 0)
+    final = pltpu.make_async_copy(gathered.at[0], inc, loc_sem.at[3])
+    final.start()
+
+    for copy in finals[2:] + [final]:
         copy.wait()
     for copy in rest[landed:]:
         copy.wait_recv()
@@ -669,9 +662,11 @@
 
 
 def deliver(inc_in, adj_in, hess_in, inc, adj, hess, first, second, third, sem):
-    held = ((inc_in, first, inc), (adj_in, second, adj), (hess_in, third, hess))
-    reads = [pltpu.make_async_copy(src, mid, sem.at[n]) for n, (src, mid, _) in enumerate(held)]
-    writes = [pltpu.make_async_copy(mid, dst, sem.at[n + 3]) for n, (_, mid, dst) in enumerate(held)]
+    held = [(inc_in.at[c], first.at[c], inc.at[c]) for c in range(2)]
+    held += [(adj_in.at[c], second.at[c], adj.at[c]) for c in range(2)]
+    held += [(hess_in, third, hess)]
+    reads = [pltpu.make_async_copy(src, mid, sem.at[n, 0]) for n, (src, mid, _) in enumerate(held)]
+    writes = [pltpu.make_async_copy(mid, dst, sem.at[n, 1]) for n, (_, mid, dst) in enumerate(held)]
     for copy in reads:
         copy.start()
     for read, write in zip(reads, writes):
@@ -702,11 +697,11 @@
         + [field] * 6
         + [state] * 6
         + halo(NZ + 8, 1) + halo(4 * NZ, 1) + halo(6 * NZ, 2) + halo(2 * NZ, 1)
-        + [pltpu.VMEM((2, ROWS, LANES), F32), pltpu.VMEM((2, 2, 1, LANES), F32)]
-        + [pltpu.VMEM((2, na, 1, LANES), F32), pltpu.VMEM((2, nb, 1, LANES), F32)]
+        + [pltpu.VMEM((ROWS, LANES), F32), pltpu.VMEM((2, 1, LANES), F32)]
+        + [pltpu.VMEM((na, 1, LANES), F32), pltpu.VMEM((nb, 1, LANES), F32)]
         + [pltpu.VMEM((2, 2, depth, rows, lanes), F32)]
         + [dma((5,)), dma((4,)), dma((4, ngz)), dma((4, ngz)), dma((4, 4)), dma((4, 4))]
-        + [dma((2, 2, max(na, nb))), dma((2, na)), dma((2, nb)), dma((4, ngz)), dma((4, ngz))]
+        + [dma((2, max(na, nb))), dma((na,)), dma((nb,)), dma((4, ngz)), dma((4, ngz))]
     )
     vmem = pl.BlockSpec(memory_space=pltpu.VMEM)
     hbm = pl.BlockSpec(memory_space=pl.ANY)
@@ -731,7 +726,7 @@
         out_shape=shapes,
         in_specs=[hbm] * 3,
         out_specs=(hbm, hbm, hbm),
-        scratch_shapes=[pltpu.VMEM(shape.shape, F32) for shape in shapes] + [dma((6,))],
+        scratch_shapes=[pltpu.VMEM(shape.shape, F32) for shape in shapes] + [dma((5, 2))],
         compiler_params=pltpu.CompilerParams(vmem_limit_bytes=62 * 1024 * 1024),
     )(*results)
 

time: 65.5 us -> 64.6 us (0.986)
  Pallas kernels: 64.7 us -> 63.8 us
    pallas_call x1, Pallas kernels: 62.6 us -> 61.8 us  [local(): pl.pallas_call(functools.partial(kernel, sizes), out_shape=shapes, in_spe...]
where the time goes in v5:
time: 64.6 us; the launch traced here: 64.4 us
  Pallas kernels  63.8 us (99%)
    pallas_call x1, Pallas kernels, local(): pl.pallas_call(functools.partial(kernel, sizes), out_shape=shapes, in_spe...  61.8 us
    pallas_call x1, Pallas kernels, local(): pl.pallas_call(deliver, out_shape=shapes, in_specs=[hbm] * 3, out_specs=(...  2 us

profile of v5, /device:TPU:2, one launch (start us, length us, event | category | flops | bytes accessed | tf_op | source)
XLA Modules:
  0.0 64.4 jit_solution(14728481509544279988)
XLA Ops:
  0.6 61.8 %shard_map.112 = (f32[2,8,64,128]{3,2,1,0:T(8,128)}, f32[2,8,64,128]{3,2,1,0:T(8,128)}, f32[64,128]{1,0:T(8,128)}) custom-call(f32[2,8,64,128]{3,2,1,0:T(8,128)} %vel_in.1, f32[8,64,128]{2,1,0:T(8,128)} %visc.1, f32[3,8,64,128]{3,2,1,0:T(8,128)} %binv.1, f32[8,64,128]{2,1,0:T(8,128)} %coup.1, f32[64,128]{1,0:T(8,128)} %fric_in.1, f32[64,128]{1,0:T(8,128)} %fstep_in.1, ...), custom_call_target="tpu_custom_call" | custom-call | tf_op jit(solution)/shard_map/pallas_call | solution.py:714
  62.4 2.0 %shard_map.113 = (f32[2,8,64,128]{3,2,1,0:T(8,128)}, f32[2,8,64,128]{3,2,1,0:T(8,128)}, f32[64,128]{1,0:T(8,128)}) custom-call(f32[2,8,64,128]{3,2,1,0:T(8,128)} %get-tuple-element.6.inc_in, f32[2,8,64,128]{3,2,1,0:T(8,128)} %get-tuple-element.7.adj_in, f32[64,128]{1,0:T(8,128)} %get-tuple-element.8.hess_in), custom_call_target="tpu_custom_call" | custom-call | tf_op jit(solution)/shard_map/pallas_call | solution.py:724

commit v6 on v5

--- a/solution.py
+++ b/solution.py
@@ -627,8 +627,15 @@
         return tuple(out)
 
     landed = len(rest)
-    basal = blocked_loop(NZ, adjoints, (blank, blank))
-    give_back(2, ZA)
+    basal = (blank, blank)
+    for o in (*range(1, ngz), 0):
+        for k in range(depth):
+            basal = adjoints(gzs[o] * depth + k, basal)
+        if o:
+            send_back(2, o, ZA.at[:, pl.ds(1 + gzs[o] * depth, depth)])
+    own = pltpu.make_async_copy(ZA.at[:, pl.ds(1 + base, depth)], places[2], loc_sem.at[2])
+    own.start()
+    finals.append(own)
     action = friction * (speed0 * basal[0] + speed1 * basal[1])
     hess[my_rows, :] = action
     vbs[0, my_rows, :] = action

time: 64.6 us -> 64.5 us (level)
  no operation moved by 1% of the time
where the time goes in v6:
time: 64.5 us; the launch traced here: 64.3 us
  Pallas kernels  63.7 us (99%)
    pallas_call x1, Pallas kernels, local(): pl.pallas_call(functools.partial(kernel, sizes), out_shape=shapes, in_spe...  61.7 us
    pallas_call x1, Pallas kernels, local(): pl.pallas_call(deliver, out_shape=shapes, in_specs=[hbm] * 3, out_specs=(...  2 us

profile of v6, /device:TPU:2, one launch (start us, length us, event | category | flops | bytes accessed | tf_op | source)
XLA Modules:
  0.0 64.3 jit_solution(13795220342779391746)
XLA Ops:
  0.6 61.7 %shard_map.112 = (f32[2,8,64,128]{3,2,1,0:T(8,128)}, f32[2,8,64,128]{3,2,1,0:T(8,128)}, f32[64,128]{1,0:T(8,128)}) custom-call(f32[2,8,64,128]{3,2,1,0:T(8,128)} %vel_in.1, f32[8,64,128]{2,1,0:T(8,128)} %visc.1, f32[3,8,64,128]{3,2,1,0:T(8,128)} %binv.1, f32[8,64,128]{2,1,0:T(8,128)} %coup.1, f32[64,128]{1,0:T(8,128)} %fric_in.1, f32[64,128]{1,0:T(8,128)} %fstep_in.1, ...), custom_call_target="tpu_custom_call" | custom-call | tf_op jit(solution)/shard_map/pallas_call | solution.py:721
  62.3 2.0 %shard_map.113 = (f32[2,8,64,128]{3,2,1,0:T(8,128)}, f32[2,8,64,128]{3,2,1,0:T(8,128)}, f32[64,128]{1,0:T(8,128)}) custom-call(f32[2,8,64,128]{3,2,1,0:T(8,128)} %get-tuple-element.6.inc_in, f32[2,8,64,128]{3,2,1,0:T(8,128)} %get-tuple-element.7.adj_in, f32[64,128]{1,0:T(8,128)} %get-tuple-element.8.hess_in), custom_call_target="tpu_custom_call" | custom-call | tf_op jit(solution)/shard_map/pallas_call | solution.py:731
